TPU v7x, 512 devices: a whole 4x8x8 slice. The times are simulated.
512 devices in a mesh: dp: 32 (over y_lo, x, core), seq: 16 (over y_hi, z).
Axes of the slice: x: 4, y: 8 (y_hi: 2, y_lo: 4; y = y_hi * 4 + y_lo), z: 8, core: 2. Of those that a mesh axis runs over, the one named last changes fastest.
Arguments:
- queries: bfloat16 [32, 2048, 1536], P('dp', 'seq'), may hold values from -120 to 120
- keys: bfloat16 [32, 2048, 1536], P('dp', 'seq'), may hold values from -4.5 to 4.5
- values: bfloat16 [32, 2048, 1536], P('dp', 'seq'), may hold values from -6 to 6
- grad_out: bfloat16 [32, 2048, 1536], P('dp', 'seq'), may hold values from -6 to 6
- conv_weight: float32 [31, 1536], replicated, may hold values from -2 to 2
- conv_bias: float32 [1536], replicated, may hold values from -4 to 4
- lengths: int32 [32], P('dp'), may hold values from 512 to 2048, as said below
Outputs:
- query_grad: bfloat16 [32, 2048, 1536], P('dp', 'seq')
- key_grad: bfloat16 [32, 2048, 1536], P('dp', 'seq')
- value_grad: bfloat16 [32, 2048, 1536], P('dp', 'seq')
- weight_grad: float32 [31, 1536], P(None, 'seq')
- bias_grad: float32 [1536], P('seq')
Inputs may be any that keep to these rules, and one draw needn't show every extreme that they name: `lengths`: each utterance's valid frames are its first ones; in every draw some utterance has all 2048 frames valid.
All inputs are finite; a program needn't handle non-finite values.
Results may differ from a plain program's by a relative error of at most 0.024.
Values may be sent and summed in bfloat16 or wider, within the bound.
A program may use at most 64 MiB of HBM per device.

v0:
```python
import math

import jax
import jax.numpy as jnp
from jax import lax
from jax.sharding import PartitionSpec as P

HEADS = 16
KERNEL = 31


masked_score = -1e30


def padded_2(block, sides, width):
    for axis, dim in sides:
        count = lax.axis_size(axis)
        forward = [(i, i + 1) for i in range(count - 1)]
        backward = [(target, source) for source, target in forward]
        low = lax.ppermute(
            lax.slice_in_dim(block, block.shape[dim] - width, None, axis=dim), axis, forward
        )
        high = lax.ppermute(lax.slice_in_dim(block, 0, width, axis=dim), axis, backward)
        block = jnp.concatenate([low, block, high], axis=dim)
    return block


def probs_block(query_block, key_heads, key_valid, score_scale):
    scores = (
        jnp.einsum("qhd,khd->hqk", query_block, key_heads, preferred_element_type=jnp.float32)
        * score_scale
    )
    scores = jnp.where(key_valid[None, None, :], scores, masked_score)
    row_top = jnp.max(scores, axis=-1, keepdims=True)
    exped = jnp.exp(scores - row_top)
    return exped / jnp.sum(exped, axis=-1, keepdims=True)


def forward_heads(query_heads, key_heads, value_heads, key_valid, block_rows, score_scale):
    seq_len, heads_here, head_dim = query_heads.shape
    blocks = query_heads.reshape(seq_len // block_rows, block_rows, heads_here, head_dim)

    def block_out(query_block):
        probs = probs_block(query_block, key_heads, key_valid, score_scale)
        return jnp.einsum(
            "hqk,khd->qhd",
            probs.astype(jnp.bfloat16),
            value_heads,
            preferred_element_type=jnp.float32,
        )

    return lax.map(block_out, blocks).reshape(seq_len, heads_here, head_dim)


def backward_heads(
    query_heads, key_heads, value_heads, grad_heads, key_valid, block_rows, score_scale
):
    seq_len, heads_here, head_dim = query_heads.shape
    count = seq_len // block_rows
    query_blocks = query_heads.reshape(count, block_rows, heads_here, head_dim)
    grad_blocks = grad_heads.reshape(count, block_rows, heads_here, head_dim)

    def block_step(carry, inputs):
        key_acc, value_acc = carry
        query_block, grad_block = inputs
        probs = probs_block(query_block, key_heads, key_valid, score_scale)
        probs_low = probs.astype(jnp.bfloat16)
        score_grad = jnp.einsum(
            "qhd,khd->hqk", grad_block, value_heads, preferred_element_type=jnp.float32
        )
        row_delta = jnp.sum(probs * score_grad, axis=-1, keepdims=True)
        diff = (probs * (score_grad - row_delta)).astype(jnp.bfloat16)
        query_part = jnp.einsum("hqk,khd->qhd", diff, key_heads, preferred_element_type=jnp.float32)
        query_part = (query_part * score_scale).astype(jnp.bfloat16)
        key_acc = key_acc + jnp.einsum(
            "hqk,qhd->khd", diff, query_block, preferred_element_type=jnp.float32
        )
        value_acc = value_acc + jnp.einsum(
            "hqk,qhd->khd", probs_low, grad_block, preferred_element_type=jnp.float32
        )
        return ((key_acc, value_acc), query_part)

    zeros = jnp.zeros((seq_len, heads_here, head_dim), jnp.float32)
    (key_acc, value_acc), query_parts = lax.scan(
        block_step, (zeros, zeros), (query_blocks, grad_blocks)
    )
    query_out = query_parts.reshape(seq_len, heads_here, head_dim)
    return (query_out, (key_acc * score_scale).astype(jnp.bfloat16), value_acc.astype(jnp.bfloat16))


def conv_forward(padded, weight, bias, count):
    conv_pre = jnp.zeros(padded[:, 0:count].shape, jnp.float32) + bias
    for j in range(KERNEL):
        conv_pre = conv_pre + weight[j] * padded[:, j : j + count]
    return conv_pre


def silu_slope(conv_pre):
    sig = jax.nn.sigmoid(conv_pre)
    return sig * (1.0 + conv_pre * (1.0 - sig))


def weight_terms(pre_grad_f, padded, count):
    return jnp.stack(
        [jnp.sum(pre_grad_f * padded[:, j : j + count], axis=(0, 1)) for j in range(KERNEL)]
    )


def transposed_conv(grad_pad, weight, count):
    rim = KERNEL // 2
    total = jnp.zeros(grad_pad[:, 0:count].shape, jnp.float32)
    for j in range(KERNEL):
        total = total + weight[j] * grad_pad[:, 2 * rim - j : 2 * rim - j + count]
    return total


def on_device(queries, keys, values, grad_out, conv_weight, conv_bias, lengths):
    seq_count = lax.axis_size("seq")
    seq_rank = lax.axis_index("seq")
    utt_count, frames, width = queries.shape
    head_dim = width // HEADS
    seq_len = frames * seq_count
    block_rows = math.gcd(seq_len, 512)
    score_scale = 1.0 / math.sqrt(head_dim)
    rim = KERNEL // 2
    positions = jnp.arange(seq_len, dtype=jnp.int32)
    key_valid = positions[None, :] < lengths[:, None]

    def split_heads(array):
        return array.reshape(utt_count, frames, HEADS, head_dim)

    query_heads, key_heads, value_heads = (
        lax.all_to_all(split_heads(queries), "seq", split_axis=2, concat_axis=1, tiled=True),
        lax.all_to_all(split_heads(keys), "seq", split_axis=2, concat_axis=1, tiled=True),
        lax.all_to_all(split_heads(values), "seq", split_axis=2, concat_axis=1, tiled=True),
    )
    outputs = [
        forward_heads(
            query_heads[0], key_heads[0], value_heads[0], key_valid[0], block_rows, score_scale
        )
    ]
    attended_heads = jnp.stack(outputs) * key_valid[:, :, None, None].astype(jnp.float32)
    attended_heads = attended_heads.astype(jnp.bfloat16)
    local_frames = seq_rank * frames + jnp.arange(frames, dtype=jnp.int32)
    local_valid = (local_frames[None, :] < lengths[:, None]).astype(jnp.float32)
    attended = lax.all_to_all(
        attended_heads, "seq", split_axis=1, concat_axis=2, tiled=True
    ).reshape(utt_count, frames, width)
    padded = padded_2(attended, (("seq", 1),), rim)
    conv_pre = conv_forward(padded, conv_weight, conv_bias, frames)
    pre_grad = (grad_out.astype(jnp.float32) * silu_slope(conv_pre)).astype(jnp.bfloat16)
    pre_grad_f = pre_grad.astype(jnp.float32)
    weight_part = weight_terms(pre_grad_f, padded, frames)
    bias_part = jnp.sum(pre_grad_f, axis=(0, 1))
    weight_share, bias_share = (
        lax.psum_scatter(
            weight_part.astype(jnp.bfloat16), "seq", scatter_dimension=1, tiled=True
        ).astype(jnp.float32),
        lax.psum_scatter(
            bias_part.astype(jnp.bfloat16), "seq", scatter_dimension=0, tiled=True
        ).astype(jnp.float32),
    )
    weight_grad, bias_grad = lax.psum((weight_share, bias_share), "dp")
    grad_pad = padded_2(pre_grad, (("seq", 1),), rim)
    attn_grad = grad_out.astype(jnp.float32) + transposed_conv(grad_pad, conv_weight, frames)
    attn_grad = (attn_grad * local_valid[:, :, None]).astype(jnp.bfloat16)
    grad_heads = lax.all_to_all(
        split_heads(attn_grad), "seq", split_axis=2, concat_axis=1, tiled=True
    )
    results = [
        backward_heads(
            query_heads[0],
            key_heads[0],
            value_heads[0],
            grad_heads[0],
            key_valid[0],
            block_rows,
            score_scale,
        )
    ]
    query_part = jnp.stack([entry[0] for entry in results])
    key_part = jnp.stack([entry[1] for entry in results])
    value_part = jnp.stack([entry[2] for entry in results])
    query_grad, key_grad, value_grad = (
        lax.all_to_all(query_part, "seq", split_axis=1, concat_axis=2, tiled=True),
        lax.all_to_all(key_part, "seq", split_axis=1, concat_axis=2, tiled=True),
        lax.all_to_all(value_part, "seq", split_axis=1, concat_axis=2, tiled=True),
    )
    query_grad = query_grad.reshape(utt_count, frames, width)
    key_grad = key_grad.reshape(utt_count, frames, width)
    value_grad = value_grad.reshape(utt_count, frames, width)
    return (query_grad, key_grad, value_grad, weight_grad, bias_grad)


def solution(mesh):
    return jax.shard_map(
        on_device,
        mesh=mesh,
        in_specs=(
            P("dp", "seq", None),
            P("dp", "seq", None),
            P("dp", "seq", None),
            P("dp", "seq", None),
            P(),
            P(),
            P("dp"),
        ),
        out_specs=(
            P("dp", "seq", None),
            P("dp", "seq", None),
            P("dp", "seq", None),
            P(None, "seq"),
            P("seq"),
        ),
        check_vma=False,
    )
```

profile of v0, /device:TPU:1, one launch (start us, length us, event | category | flops | bytes accessed | tf_op | source)
XLA Modules:
  0.0 778.7 jit_solution(3893358324005687875)
XLA Ops:
  9.1 16.2 %all-to-all-start = ((bf16[1,128,16,96]{1,3,0,2:T(8,128)(2,1)}), bf16[1,128,16,96]{1,3,0,2:T(8,128)(2,1)S(1)}, u32[]{:S(2)}, u32[]{:S(2)}) async-start(bf16[1,128,16,96]{1,3,0,2:T(8,128)(2,1)} %bitcast.1), calls=%async_computation | async-start | bytes 786432 | tf_op jit(solution)/shard_map/all_to_all | solution.py:133
  27.2 10.9 %all-to-all-done = bf16[1,128,16,96]{1,3,0,2:T(8,128)(2,1)S(1)} async-done(((bf16[1,128,16,96]{1,3,0,2:T(8,128)(2,1)}), bf16[1,128,16,96]{1,3,0,2:T(8,128)(2,1)S(1)}, u32[]{:S(2)}, u32[]{:S(2)}) %all-to-all-start) | async-done | bytes 393248 | tf_op jit(solution)/shard_map/all_to_all | solution.py:133
  38.1 8.7 %all-to-all-start.1 = ((bf16[1,128,16,96]{1,3,0,2:T(8,128)(2,1)}), bf16[1,128,16,96]{1,3,0,2:T(8,128)(2,1)S(1)}, u32[]{:S(2)}, u32[]{:S(2)}) async-start(bf16[1,128,16,96]{1,3,0,2:T(8,128)(2,1)} %bitcast.5), calls=%async_computation.1 | async-start | bytes 786432 | tf_op jit(solution)/shard_map/all_to_all | solution.py:134
  48.8 11.1 %all-to-all-done.1 = bf16[1,128,16,96]{1,3,0,2:T(8,128)(2,1)S(1)} async-done(((bf16[1,128,16,96]{1,3,0,2:T(8,128)(2,1)}), bf16[1,128,16,96]{1,3,0,2:T(8,128)(2,1)S(1)}, u32[]{:S(2)}, u32[]{:S(2)}) %all-to-all-start.1) | async-done | bytes 393248 | tf_op jit(solution)/shard_map/all_to_all | solution.py:134
  59.9 8.5 %all-to-all-start.2 = ((bf16[1,128,16,96]{1,3,0,2:T(8,128)(2,1)}), bf16[1,128,16,96]{1,3,0,2:T(8,128)(2,1)S(1)}, u32[]{:S(2)}, u32[]{:S(2)}) async-start(bf16[1,128,16,96]{1,3,0,2:T(8,128)(2,1)} %bitcast.9), calls=%async_computation.2 | async-start | bytes 786432 | tf_op jit(solution)/shard_map/all_to_all | solution.py:135
  69.8 11.6 %all-to-all-done.2 = bf16[1,128,16,96]{1,3,0,2:T(8,128)(2,1)S(1)} async-done(((bf16[1,128,16,96]{1,3,0,2:T(8,128)(2,1)}), bf16[1,128,16,96]{1,3,0,2:T(8,128)(2,1)S(1)}, u32[]{:S(2)}, u32[]{:S(2)}) %all-to-all-start.2) | async-done | bytes 393248 | tf_op jit(solution)/shard_map/all_to_all | solution.py:135
  81.7 23.5 %while.26 = (s32[]{:T(128)}, f32[4,512,1,96]{1,0,3,2:T(4,128)S(1)}, bf16[4,512,1,96]{1,3,2,0:T(8,128)(2,1)S(1)}, bf16[2048,1,96]{0,2,1:T(8,128)(2,1)S(1)}, bf16[...) while((s32[]{:T(128)}, f32[4,512,1,96]{1,0,3,2:T(4,128)S(1)}, ...), condition=%wide.region_3.4_spmd.clone, body=%wide.region_0.3_spmd.clone.sunk | while | flops 415237120 | bytes 14469217 | solution.py:52
  107.4 11.6 %reduce.77 = bf16[2048,96]{1,0:T(8,128)(2,1)S(1)} reduce(bf16[2048,1,1,96]{3,2,1,0:T(2,128)(2,1)S(1)} %bitcast.214, bf16[]{:T(256)} %broadcast.206), dimensions={1,2}, to_apply=%bitcast.152.reduce_sub_computation | reduce | bytes 786434
  120.6 8.9 %all-to-all-start.3 = ((bf16[16,2,6144]{2,1,0:T(2,128)(2,1)}), bf16[16,2,6144]{2,1,0:T(2,128)(2,1)S(1)}, u32[]{:S(2)}, u32[]{:S(2)}) async-start(bf16[16,2,6144]{2,1,0:T(2,128)(2,1)} %reshape.396), calls=%async_computation.3 | async-start | bytes 786432 | tf_op jit(solution)/shard_map/all_to_all | solution.py:146
  130.4 12.0 %all-to-all-done.3 = bf16[16,2,6144]{2,1,0:T(2,128)(2,1)S(1)} async-done(((bf16[16,2,6144]{2,1,0:T(2,128)(2,1)}), bf16[16,2,6144]{2,1,0:T(2,128)(2,1)S(1)}, u32[]{:S(2)}, u32[]{:S(2)}) %all-to-all-start.3) | async-done | bytes 393248 | tf_op jit(solution)/shard_map/all_to_all | solution.py:146
  151.3 3.9 collective-permute-done.1
  155.2 18.0 %fusion.182 = (bf16[1536]{0:T(1024)(128)(2,1)}, bf16[1,128,1536]{1,2,0:T(8,128)(2,1)S(1)}) fusion(bf16[1,15,1536]{1,2,0:T(8,128)(2,1)S(1)} %collective-permute-done.1, bf16[1,128,1536]{1,2,0:T(8,128)(2,1)S(1)} %bitcast.209, f32[1536]{0:T(1024)} %get-tuple-element.278, f32[1536]{0:T(1024)} %get-tuple-element.279, f32[1536]{0:T(1024)S(1)} %get-tuple-element.250, ...), kind=kLoop, calls=%fused_computation.409 | loop fusion | flops 38140416 | bytes 1471488 | tf_op jit(solution)/shard_map/reduce_sum | solution.py:154
  174.7 4.3 collective-permute-start.3
  183.7 16.7 %fusion.45 = bf16[1,128,1536]{1,2,0:T(8,128)(2,1)} fusion(bf16[1,128,1536]{1,2,0:T(8,128)(2,1)S(1)} %copy.94, bf16[1,128,1536]{1,2,0:T(8,128)(2,1)S(1)} %get-tuple-element.313, bf16[1,15,1536]{1,2,0:T(8,128)(2,1)S(1)} %collective-permute-done.3, bf16[1,15,1536]{1,2,0:T(8,128)(2,1)S(1)} %collective-permute-done.2, f32[128]{0:T(128)S(1)} %compare_convert_fusion, ...), kind=kLoop, calls=%fused_computation.231 | loop fusion | flops 36569088 | bytes 1462784 | tf_op jit(solution)/shard_map/convert_element_type | solution.py:166
  200.4 22.6 %all-to-all-start.4 = ((bf16[1,128,16,96]{1,3,0,2:T(8,128)(2,1)}), bf16[1,128,16,96]{1,3,0,2:T(8,128)(2,1)S(1)}, u32[]{:S(2)}, u32[]{:S(2)}) async-start(bf16[1,128,16,96]{1,3,0,2:T(8,128)(2,1)} %bitcast.16), calls=%async_computation.4 | async-start | bytes 786432 | tf_op jit(solution)/shard_map/all_to_all | solution.py:167
  223.1 12.4 %all-to-all-done.4 = bf16[1,128,16,96]{1,3,0,2:T(8,128)(2,1)S(1)} async-done(((bf16[1,128,16,96]{1,3,0,2:T(8,128)(2,1)}), bf16[1,128,16,96]{1,3,0,2:T(8,128)(2,1)S(1)}, u32[]{:S(2)}, u32[]{:S(2)}) %all-to-all-start.4) | async-done | bytes 393248 | tf_op jit(solution)/shard_map/all_to_all | solution.py:167
  236.6 57.4 %while.27 = (s32[]{:T(128)}, f32[2048,1,96]{0,2,1:T(8,128)S(1)}, f32[2048,1,96]{0,2,1:T(8,128)}, bf16[4,512,1,96]{1,3,2,0:T(8,128)(2,1)}, bf16[4,512,1,96]{1,3,2...) while((s32[]{:T(128)}, f32[2048,1,96]{0,2,1:T(8,128)S(1)}, ...), condition=%wide.region_8.9_spmd.clone, body=%wide.region_4.0_spmd.clone.sunk | while | flops 1033732608 | bytes 81923864 | solution.py:84
  241.1 3.7 fusion.216
  255.5 3.7 fusion.216
  269.8 3.7 fusion.216
  284.2 3.7 fusion.216
  296.0 11.8 %reduce.80 = bf16[2048,96]{1,0:T(8,128)(2,1)S(1)} reduce(bf16[2048,1,1,96]{3,2,1,0:T(2,128)(2,1)S(1)} %bitcast.217, bf16[]{:T(256)} %broadcast.206), dimensions={1,2}, to_apply=%bitcast.158.reduce_sub_computation | reduce | bytes 786434
  309.4 5.0 all-to-all-start.7
  315.2 11.6 %reduce.79 = bf16[2048,96]{1,0:T(8,128)(2,1)S(1)} reduce(bf16[2048,1,1,96]{3,2,1,0:T(2,128)(2,1)S(1)} %bitcast.218, bf16[]{:T(256)} %broadcast.206), dimensions={1,2}, to_apply=%bitcast.156.reduce_sub_computation | reduce | bytes 786434
  328.4 11.6 %all-to-all-start.6 = ((bf16[16,2,6144]{2,1,0:T(2,128)(2,1)}), bf16[16,2,6144]{2,1,0:T(2,128)(2,1)S(1)}, u32[]{:S(2)}, u32[]{:S(2)}) async-start(bf16[16,2,6144]{2,1,0:T(2,128)(2,1)} %reshape.400), calls=%async_computation.6 | async-start | bytes 786432 | tf_op jit(solution)/shard_map/all_to_all | solution.py:186
  340.1 3.9 fusion.123
  356.7 11.6 %reduce.78 = bf16[2048,96]{1,0:T(8,128)(2,1)S(1)} reduce(bf16[2048,1,1,96]{3,2,1,0:T(2,128)(2,1)S(1)} %bitcast.215, bf16[]{:T(256)} %broadcast.206), dimensions={1,2}, to_apply=%bitcast.154.reduce_sub_computation | reduce | bytes 786434
  369.9 11.6 %all-to-all-start.5 = ((bf16[16,2,6144]{2,1,0:T(2,128)(2,1)}), bf16[16,2,6144]{2,1,0:T(2,128)(2,1)S(1)}, u32[]{:S(2)}, u32[]{:S(2)}) async-start(bf16[16,2,6144]{2,1,0:T(2,128)(2,1)} %reshape.398), calls=%async_computation.5 | async-start | bytes 786432 | tf_op jit(solution)/shard_map/all_to_all | solution.py:185
  381.5 4.1 fusion.107
  393.9 46.9 %all-reduce = bf16[1536]{0:T(1024)(128)(2,1)S(1)} all-reduce(bf16[1536]{0:T(1024)(128)(2,1)} %get-tuple-element.312), channel_id=3, replica_groups=mesh['dp'=32,'seq'=16] {'seq'}, use_global_device_ids=true, to_apply=%region_43.44.clone | all-reduce | flops 1536 | bytes 6144
  440.9 187.8 %reduce-scatter.4.cloned.1.call-done = bf16[96,31]{1,0:T(8,128)(2,1)} async-done(((bf16[1536,31]{1,0:T(8,128)(2,1)}), bf16[96,31]{1,0:T(8,128)(2,1)}) %reduce-scatter.4.cloned.1.call-update) | async-done | bytes 5968
  629.5 132.7 %all-reduce.1 = (f32[31,96]{1,0:T(8,128)}, f32[96]{0:T(128)}) all-reduce(bf16[31,96]{1,0:T(8,128)(2,1)S(1)} %copy.122, f32[96]{0:T(128)S(1)} %dynamic-slice_convert_fusion), channel_id=1, replica_groups=mesh['dp'=32,'seq'=16] {'dp'}, use_global_device_ids=true, to_apply=%region_41.42 | all-reduce | flops 3072 | bytes 18624 | tf_op jit(solution)/shard_map/psum | solution.py:163
  (211 shorter events, 130.9 us)
Async XLA Ops:
  9.1 29.0 %all-to-all-start = ((bf16[1,128,16,96]{1,3,0,2:T(8,128)(2,1)}), bf16[1,128,16,96]{1,3,0,2:T(8,128)(2,1)S(1)}, u32[]{:S(2)}, u32[]{:S(2)}) async-start(bf16[1,128,16,96]{1,3,0,2:T(8,128)(2,1)} %bitcast.1), calls=%async_computation | async-start | bytes 786432 | tf_op jit(solution)/shard_map/all_to_all | solution.py:133
  38.1 21.7 %all-to-all-start.1 = ((bf16[1,128,16,96]{1,3,0,2:T(8,128)(2,1)}), bf16[1,128,16,96]{1,3,0,2:T(8,128)(2,1)S(1)}, u32[]{:S(2)}, u32[]{:S(2)}) async-start(bf16[1,128,16,96]{1,3,0,2:T(8,128)(2,1)} %bitcast.5), calls=%async_computation.1 | async-start | bytes 786432 | tf_op jit(solution)/shard_map/all_to_all | solution.py:134
  59.9 21.5 %all-to-all-start.2 = ((bf16[1,128,16,96]{1,3,0,2:T(8,128)(2,1)}), bf16[1,128,16,96]{1,3,0,2:T(8,128)(2,1)S(1)}, u32[]{:S(2)}, u32[]{:S(2)}) async-start(bf16[1,128,16,96]{1,3,0,2:T(8,128)(2,1)} %bitcast.9), calls=%async_computation.2 | async-start | bytes 786432 | tf_op jit(solution)/shard_map/all_to_all | solution.py:135
  105.3 24.2 %copy-start.9 = (f32[31,1536]{1,0:T(8,128)S(1)}, f32[31,1536]{1,0:T(8,128)}, u32[]{:S(2)}) copy-start(f32[31,1536]{1,0:T(8,128)} %param.15) | copy-start | bytes 571396
  119.0 30.9 %copy-start.6 = (bf16[1,128,1536]{2,1,0:T(8,128)(2,1)S(1)}, bf16[1,128,1536]{2,1,0:T(8,128)(2,1)}, u32[]{:S(2)}) copy-start(bf16[1,128,1536]{2,1,0:T(8,128)(2,1)} %param.14) | copy-start | bytes 1179652
  120.6 21.8 %all-to-all-start.3 = ((bf16[16,2,6144]{2,1,0:T(2,128)(2,1)}), bf16[16,2,6144]{2,1,0:T(2,128)(2,1)S(1)}, u32[]{:S(2)}, u32[]{:S(2)}) async-start(bf16[16,2,6144]{2,1,0:T(2,128)(2,1)} %reshape.396), calls=%async_computation.3 | async-start | bytes 786432 | tf_op jit(solution)/shard_map/all_to_all | solution.py:146
  144.2 7.0 collective-permute-start
  146.6 8.6 %collective-permute-start.1 = (bf16[1,15,1536]{1,2,0:T(8,128)(2,1)S(1)}, bf16[1,15,1536]{1,2,0:T(8,128)(2,1)S(1)}, u32[]{:S(2)}, u32[]{:S(2)}) collective-permute-start(bf16[1,15,1536]{1,2,0:T(8,128)(2,1)S(1)} %get-tuple-element.323), channel_id=1, source_target_pairs={{1,0},{2,1},{3,2},{4,3},{5,4},{6,5},{7,6},{8,7},{9,8},{10,9},{11,1... | collective-permute-start | bytes 138248 | tf_op jit(solution)/shard_map/ppermute | solution.py:23
  155.2 45.3 %copy-start.2 = (bf16[1,15,1536]{1,2,0:T(8,128)(2,1)}, bf16[1,15,1536]{1,2,0:T(8,128)(2,1)S(1)}, u32[]{:S(2)}) copy-start(bf16[1,15,1536]{1,2,0:T(8,128)(2,1)S(1)} %collective-permute-done.1) | copy-start | bytes 138244
  173.4 8.8 %collective-permute-start.2 = (bf16[1,15,1536]{1,2,0:T(8,128)(2,1)S(1)}, bf16[1,15,1536]{1,2,0:T(8,128)(2,1)S(1)}, u32[]{:S(2)}, u32[]{:S(2)}) collective-permute-start(bf16[1,15,1536]{1,2,0:T(8,128)(2,1)S(1)} %get-tuple-element.320), channel_id=1, source_target_pairs={{1,0},{2,1},{3,2},{4,3},{5,4},{6,5},{7,6},{8,7},{9,8},{10,9},{11,1... | collective-permute-start | bytes 138248 | tf_op jit(solution)/shard_map/ppermute | solution.py:23
  174.7 9.0 %collective-permute-start.3 = (bf16[1,15,1536]{1,2,0:T(8,128)(2,1)S(1)}, bf16[1,15,1536]{1,2,0:T(8,128)(2,1)S(1)}, u32[]{:S(2)}, u32[]{:S(2)}) collective-permute-start(bf16[1,15,1536]{1,2,0:T(8,128)(2,1)S(1)} %get-tuple-element.321), channel_id=1, source_target_pairs={{0,1},{1,2},{2,3},{3,4},{4,5},{5,6},{6,7},{7,8},{8,9},{9,10},{10,1... | collective-permute-start | bytes 138248 | tf_op jit(solution)/shard_map/ppermute | solution.py:20
  200.4 35.1 %all-to-all-start.4 = ((bf16[1,128,16,96]{1,3,0,2:T(8,128)(2,1)}), bf16[1,128,16,96]{1,3,0,2:T(8,128)(2,1)S(1)}, u32[]{:S(2)}, u32[]{:S(2)}) async-start(bf16[1,128,16,96]{1,3,0,2:T(8,128)(2,1)} %bitcast.16), calls=%async_computation.4 | async-start | bytes 786432 | tf_op jit(solution)/shard_map/all_to_all | solution.py:167
  237.3 3.8 copy-start.4
  241.1 3.7 copy-start.1
  241.1 3.7 copy-start.8
  244.8 2.6 copy-start.5
  251.6 3.8 copy-start.4
  255.4 3.7 copy-start.1
  255.5 3.7 copy-start.8
  266.0 3.8 copy-start.4
  269.8 3.7 copy-start.1
  269.8 3.7 copy-start.8
  280.4 3.8 copy-start.4
  284.2 3.7 copy-start.1
  284.2 3.7 copy-start.8
  296.0 44.0 %copy-start.3 = (bf16[1,15,1536]{1,2,0:T(8,128)(2,1)S(1)}, bf16[1,15,1536]{1,2,0:T(8,128)(2,1)}, u32[]{:S(2)}) copy-start(bf16[1,15,1536]{1,2,0:T(8,128)(2,1)} %copy-done.2) | copy-start | bytes 138244
  309.4 19.0 %all-to-all-start.7 = ((bf16[16,2,6144]{2,1,0:T(2,128)(2,1)}), bf16[16,2,6144]{2,1,0:T(2,128)(2,1)}, u32[]{:S(2)}, u32[]{:S(2)}) async-start(bf16[16,2,6144]{2,1,0:T(2,128)(2,1)} %reshape.402), calls=%async_computation.7 | async-start | bytes 786432 | tf_op jit(solution)/shard_map/all_to_all | solution.py:187
  328.4 41.4 %all-to-all-start.6 = ((bf16[16,2,6144]{2,1,0:T(2,128)(2,1)}), bf16[16,2,6144]{2,1,0:T(2,128)(2,1)S(1)}, u32[]{:S(2)}, u32[]{:S(2)}) async-start(bf16[16,2,6144]{2,1,0:T(2,128)(2,1)} %reshape.400), calls=%async_computation.6 | async-start | bytes 786432 | tf_op jit(solution)/shard_map/all_to_all | solution.py:186
  368.2 20.2 %copy-start.10 = (bf16[1,1536]{1,0:T(2,128)(2,1)S(1)}, bf16[1,1536]{1,0:T(2,128)(2,1)}, u32[]{:S(2)}) copy-start(bf16[1,1536]{1,0:T(2,128)(2,1)} %stack.164) | copy-start | bytes 9220
  368.3 20.2 %copy-start.11 = (bf16[1,1536]{1,0:T(2,128)(2,1)S(1)}, bf16[1,1536]{1,0:T(2,128)(2,1)}, u32[]{:S(2)}) copy-start(bf16[1,1536]{1,0:T(2,128)(2,1)} %stack.165) | copy-start | bytes 9220
  369.9 399.0 %all-to-all-start.5 = ((bf16[16,2,6144]{2,1,0:T(2,128)(2,1)}), bf16[16,2,6144]{2,1,0:T(2,128)(2,1)S(1)}, u32[]{:S(2)}, u32[]{:S(2)}) async-start(bf16[16,2,6144]{2,1,0:T(2,128)(2,1)} %reshape.398), calls=%async_computation.5 | async-start | bytes 786432 | tf_op jit(solution)/shard_map/all_to_all | solution.py:185
  381.4 247.2 %reduce-scatter.4.cloned.1.call-start = ((), (), s32[]{:S(2)}) async-start(), calls=%async_computation.9 | async-start | bytes 417792
  (8 other events, 16.1 us)
Sparse Core Ops, SparseCore 0:
  392.1 236.5 reduce-scatter.3
where the time goes:
time: 793 us; the launch traced here: 779 us
  waiting for transfers between devices  255 us (32%)
  blocking collectives  180 us (23%)
  other arithmetic  115 us (15%)
  starting transfers between devices  102 us (13%)
  local copies, waits for them, and re-layouts  63.7 us (8%)
  matrix products  45.2 us (6%)
  between operations  16.5 us (2%)
    unnamed x2, waiting for transfers between devices  188 us
    psum x1, blocking collectives, on_device(): weight_grad, bias_grad = lax.psum((weight_share, bias_share), 'dp')  133 us
    unnamed x1, blocking collectives  46.9 us
    unnamed x6, other arithmetic  46.6 us
    unnamed x39, local copies, waits for them, and re-layouts  24.8 us
    all_to_all x1, starting transfers between devices, on_device(): lax.all_to_all(split_heads(attn_grad), 'seq', split_axis=2, concat_axis=1...  22.6 us
    reduce_sum x1, other arithmetic, on_device(): bias_part = jnp.sum(pre_grad_f, axis=(0, 1))  18 us
    convert_element_type x1, other arithmetic, on_device(): attn_grad = (attn_grad * local_valid[:, :, None]).astype(jnp.bfloat16)  16.7 us
  transfers between devices with their start and end apart: 13, of which 10 were waited for; matrix products, arithmetic and copies ran while one was open for 9% of the time, Pallas kernels for 0%

commit v1 on v0

v1 whole, which is shorter than its diff:
```python
import math

import jax
import jax.numpy as jnp
from jax import lax
from jax.experimental import pallas as pl
from jax.experimental.pallas import tpu as pltpu
from jax.sharding import PartitionSpec as P

MESH = pl.DeviceIdType.MESH
HEADS = 16
KERNEL = 31
RIM = KERNEL // 2
HEAD = 96
WIDE = 128
PAD = 16
ROWS = 256
CONV = 128
NEG = -1e30
F32 = jnp.float32
BF16 = jnp.bfloat16
NT = (((1,), (1,)), ((), ()))


def core(
    q_hbm, k_hbm, v_hbm, g_hbm, weight_ref, bias_ref, length_ref,
    dq_ref, dk_ref, dv_ref, dw_ref, db_ref,
    raw, stage, q_t, k_t, v_t, g_t, weights, low, att, out_nat, slope, pre, upper,
    grad_x, grad_t, stage_out, back, tap_sum, one, two, three,
    load_sem, own_sem, send_sem, recv_sem, sum_send, sum_recv,
):
    seq_len = q_t.shape[1]
    frames = raw.shape[1]
    width = raw.shape[2]
    me = lax.axis_index("seq")
    dp = lax.axis_index("dp")
    dp_core = lax.rem(dp, 2)
    dp_x = lax.rem(dp // 2, 4)
    dp_y = dp // 8
    length = length_ref[0]

    sources = (k_hbm, q_hbm, v_hbm, g_hbm)
    loads = [
        pltpu.make_async_copy(ref.at[0], raw.at[i], load_sem.at[i])
        for i, ref in enumerate(sources)
    ]
    for load in loads:
        load.start()
    seq_peers = [lax.rem(me + step, HEADS) for step in range(1, HEADS)]
    core_peers = [dp_y * 8 + dp_x * 2 + 1 - dp_core]
    x_peers = [dp_y * 8 + lax.rem(dp_x + s, 4) * 2 + dp_core for s in (1, 2, 3)]
    y_peers = [lax.rem(dp_y + s, 4) * 8 + dp_x * 2 + dp_core for s in (1, 2, 3)]
    barrier = pltpu.get_barrier_semaphore()
    for peer in seq_peers:
        pl.semaphore_signal(barrier, inc=1, device_id={"seq": peer}, device_id_type=MESH)
    for peer in core_peers + x_peers + y_peers:
        pl.semaphore_signal(barrier, inc=1, device_id={"dp": peer}, device_id_type=MESH)

    k_t[HEAD:, :] = jnp.zeros((WIDE - HEAD, seq_len), BF16)
    key_pos = lax.broadcasted_iota(jnp.int32, (16, seq_len), 1)
    key_row = lax.broadcasted_iota(jnp.int32, (16, seq_len), 0)
    mask = jnp.where((key_row == 0) & (key_pos >= length), F32(NEG), F32(0.0))
    k_t[HEAD : HEAD + 16, :] = mask.astype(BF16)
    q_t[HEAD:, :] = jnp.zeros((WIDE - HEAD, seq_len), BF16)
    q_t[HEAD : HEAD + 16, :] = jnp.where(key_row == 0, F32(1.0), F32(0.0)).astype(BF16)
    v_t[HEAD:, :] = jnp.zeros((WIDE - HEAD, seq_len), BF16)
    v_t[HEAD : HEAD + 16, :] = jnp.where(key_row < 3, F32(1.0), F32(0.0)).astype(BF16)
    g_t[HEAD:, :] = jnp.zeros((WIDE - HEAD, seq_len), BF16)
    first = pl.multiple_of((me * HEAD) // WIDE * WIDE, WIDE)
    second = pl.multiple_of(jnp.minimum((me * HEAD) // WIDE + 1, width // WIDE - 1) * WIDE, WIDE)

    def own_columns(ref):
        both = jnp.concatenate([ref[:, pl.ds(first, WIDE)], ref[:, pl.ds(second, WIDE)]], axis=1)
        part = both[:, 0:HEAD]
        for turn in range(1, 4):
            at = turn * HEAD % WIDE
            part = jnp.where(lax.rem(me, 4) == turn, both[:, at : at + HEAD], part)
        return part

    weights[...] = jnp.zeros(weights.shape, F32)
    weights[0:KERNEL, 0:HEAD] = own_columns(weight_ref)
    weights[KERNEL : KERNEL + 1, 0:HEAD] = own_columns(bias_ref)
    zero_rim = jnp.zeros((PAD, WIDE), F32)
    for buffer in (att, pre):
        buffer[0:PAD, :] = zero_rim
        buffer[PAD + seq_len :, :] = zero_rim
    tap_sum[...] = jnp.zeros(tap_sum.shape, F32)

    pl.semaphore_wait(barrier, 2 * HEADS - 10)

    own_lanes = pl.ds(pl.multiple_of(me * frames, frames), frames)
    own_rows = pl.ds(pl.multiple_of(me * HEAD, HEAD), HEAD)
    landings = (k_t, q_t, v_t, g_t)
    kept = []
    for i, landing in enumerate(landings):
        loads[i].wait()
        for b in range(width // WIDE):
            stage[i, b * WIDE : (b + 1) * WIDE, :] = raw[i, :, b * WIDE : (b + 1) * WIDE].T
        target = landing.at[pl.ds(0, HEAD), own_lanes]
        for peer in seq_peers:
            pltpu.make_async_remote_copy(
                src_ref=stage.at[i, pl.ds(pl.multiple_of(peer * HEAD, HEAD), HEAD), :],
                dst_ref=target,
                send_sem=send_sem.at[i],
                recv_sem=recv_sem.at[i],
                device_id={"seq": peer},
                device_id_type=MESH,
            ).start()
        keep = pltpu.make_async_copy(stage.at[i, own_rows, :], target, own_sem.at[i])
        keep.start()
        kept.append(keep)

    def arrived(i):
        kept[i].wait()
        whole = landings[i].at[pl.ds(0, HEAD), pl.ds(0, seq_len - frames)]
        pltpu.make_async_copy(whole, whole, recv_sem.at[i]).wait()

    arrived(0)
    arrived(1)
    arrived(2)

    rate = F32(math.log2(math.e) / math.sqrt(HEAD))

    def forward(step, _):
        at = pl.multiple_of(step * ROWS, ROWS)
        rows = pl.ds(at, ROWS)
        query = q_t[:, rows].T
        scores = jnp.dot(query, k_t[...], preferred_element_type=F32)
        top = jnp.max(scores, axis=1, keepdims=True)
        exped = jnp.exp2((scores - top) * rate).astype(BF16)
        low[rows, :] = exped
        out_t = lax.dot_general(v_t[...], exped, NT, preferred_element_type=F32)
        out = out_t.T
        total = out[:, HEAD : HEAD + 1]
        upper[rows, :] = jnp.broadcast_to(1.0 / total, (ROWS, WIDE))
        out = out * (1.0 / total)
        out_nat[rows, :] = out
        place = at + lax.broadcasted_iota(jnp.int32, (ROWS, WIDE), 0)
        lane = lax.broadcasted_iota(jnp.int32, (ROWS, WIDE), 1)
        shown = jnp.where((place < length) & (lane < HEAD), out, 0.0)
        att[pl.ds(pl.multiple_of(PAD + at, PAD), ROWS), :] = shown.astype(BF16).astype(F32)
        return 0

    lax.fori_loop(0, seq_len // ROWS, forward, 0)

    def conv(step, _):
        at = pl.multiple_of(step * CONV, CONV)
        window = att[pl.ds(at, CONV + 2 * PAD), :]
        total = jnp.broadcast_to(weights[KERNEL : KERNEL + 1, :], (CONV, WIDE))
        for j in range(KERNEL):
            total = total + weights[j : j + 1, :] * window[j + 1 : j + 1 + CONV, :]
        sig = jax.nn.sigmoid(total)
        slope[pl.ds(at, CONV), :] = sig * (1.0 + total * (1.0 - sig))
        return 0

    lax.fori_loop(0, seq_len // CONV, conv, 0)
    arrived(3)

    def gate(step, _):
        at = pl.multiple_of(step * CONV, CONV)
        rows = pl.ds(at, CONV)
        grad = g_t[:, rows].T.astype(F32)
        gated = (grad * slope[rows, :]).astype(BF16).astype(F32)
        pre[pl.ds(pl.multiple_of(PAD + at, PAD), CONV), :] = gated
        return 0

    lax.fori_loop(0, seq_len // CONV, gate, 0)

    def conv_back(step, _):
        at = pl.multiple_of(step * CONV, CONV)
        rows = pl.ds(at, CONV)
        window = pre[pl.ds(at, CONV + 2 * PAD), :]
        total = g_t[:, rows].T.astype(F32)
        for j in range(KERNEL):
            shift = PAD + RIM - j
            total = total + weights[j : j + 1, :] * window[shift : shift + CONV, :]
        place = at + lax.broadcasted_iota(jnp.int32, (CONV, WIDE), 0)
        lane = lax.broadcasted_iota(jnp.int32, (CONV, WIDE), 1)
        total = jnp.where((place < length) & (lane < HEAD), total, 0.0).astype(BF16).astype(F32)
        scaled = (total * upper[rows, :]).astype(BF16).astype(F32)
        delta = -jnp.sum(scaled * out_nat[rows, :], axis=1, keepdims=True)
        high = delta.astype(BF16).astype(F32)
        middle = (delta - high).astype(BF16).astype(F32)
        last = delta - high - middle
        scaled = jnp.where(lane == HEAD, high, scaled)
        scaled = jnp.where(lane == HEAD + 1, middle, scaled)
        scaled = jnp.where(lane == HEAD + 2, last, scaled).astype(BF16)
        grad_x[rows, :] = scaled
        grad_t[:, rows] = scaled.T
        return 0

    lax.fori_loop(0, seq_len // CONV, conv_back, 0)

    out_sent = [len(landings) + i for i in range(3)]

    def send_back(which, step):
        for part in range(ROWS // frames):
            peer = step * (ROWS // frames) + part
            source = stage_out.at[which, pl.ds(pl.multiple_of(peer * HEAD, HEAD), HEAD), :]
            target = back.at[which, own_rows, :]

            @pl.when(peer != me)
            def _():
                pltpu.make_async_remote_copy(
                    src_ref=source,
                    dst_ref=target,
                    send_sem=send_sem.at[out_sent[which]],
                    recv_sem=recv_sem.at[out_sent[which]],
                    device_id={"seq": peer},
                    device_id_type=MESH,
                ).start()

    def put(which, step, block):
        for part in range(ROWS // frames):
            peer = step * (ROWS // frames) + part
            piece = block[:, part * frames : (part + 1) * frames]
            stage_out[which, pl.ds(pl.multiple_of(peer * HEAD, HEAD), HEAD), :] = piece
        send_back(which, step)

    steps = seq_len // ROWS
    turned = me // (ROWS // frames)

    def value_step(step, _):
        step = lax.rem(step + turned, steps)
        columns = pl.ds(pl.multiple_of(step * ROWS, ROWS), ROWS)
        block = jnp.dot(grad_t[0:HEAD, :], low[:, columns], preferred_element_type=F32)
        put(2, step, block.astype(BF16))
        return 0

    lax.fori_loop(0, steps, value_step, 0)

    def taps(step, _):
        at = pl.multiple_of(step * CONV, CONV)
        window = att[pl.ds(at, CONV + 2 * PAD), :]
        gated = pre[pl.ds(pl.multiple_of(PAD + at, PAD), CONV), :]
        for j in range(KERNEL):
            term = gated * window[j + 1 : j + 1 + CONV, :]
            tap_sum[j] += jnp.sum(term.reshape(CONV // 8, 8, WIDE), axis=0)
        tap_sum[KERNEL] += jnp.sum(gated.reshape(CONV // 8, 8, WIDE), axis=0)
        return 0

    lax.fori_loop(0, seq_len // CONV, taps, 0)

    def sum_start(level, slots, mine, peers, value):
        slots[mine] = value
        for peer in peers:
            pltpu.make_async_remote_copy(
                src_ref=slots.at[mine],
                dst_ref=slots.at[mine],
                send_sem=sum_send.at[level],
                recv_sem=sum_recv.at[level],
                device_id={"dp": peer},
                device_id_type=MESH,
            ).start()

    def sum_end(level, slots, peers):
        whole = slots.at[pl.ds(0, len(peers))]
        pltpu.make_async_copy(whole, whole, sum_recv.at[level]).wait()
        value = slots[0]
        for i in range(1, len(peers) + 1):
            value = value + slots[i]
        return value

    sum_start(0, one, dp_core, core_peers, jnp.sum(tap_sum[...], axis=1))

    back_scale = F32(1.0 / math.sqrt(HEAD))

    def query_step(step, _):
        step = lax.rem(step + turned, steps)
        rows = pl.ds(pl.multiple_of(step * ROWS, ROWS), ROWS)
        change = jnp.dot(grad_x[rows, :], v_t[...], preferred_element_type=F32)
        diff = (change * low[rows, :].astype(F32)).astype(BF16)
        low[rows, :] = diff
        block = lax.dot_general(k_t[0:HEAD, :], diff, NT, preferred_element_type=F32)
        put(0, step, (block * back_scale).astype(BF16))
        return 0

    lax.fori_loop(0, steps, query_step, 0)
    sum_start(1, two, dp_x, x_peers, sum_end(0, one, core_peers))

    def key_step(step, _):
        step = lax.rem(step + turned, steps)
        columns = pl.ds(pl.multiple_of(step * ROWS, ROWS), ROWS)
        block = jnp.dot(q_t[0:HEAD, :], low[:, columns], preferred_element_type=F32)
        put(1, step, (block * back_scale).astype(BF16))
        return 0

    lax.fori_loop(0, steps, key_step, 0)
    sum_start(2, three, dp_y, y_peers, sum_end(1, two, x_peers))
    sums = sum_end(2, three, y_peers)
    dw_ref[...] = sums[0:KERNEL, 0:HEAD]
    db_ref[...] = sums[KERNEL : KERNEL + 1, 0:HEAD]

    others = pl.ds(0, (HEADS - 1) * HEAD)
    for which, result in ((2, dv_ref), (0, dq_ref), (1, dk_ref)):
        back[which, own_rows, :] = stage_out[which, own_rows, :]
        whole = back.at[which, others, :]
        pltpu.make_async_copy(whole, whole, recv_sem.at[out_sent[which]]).wait()
        for b in range(width // WIDE):
            result[0, :, b * WIDE : (b + 1) * WIDE] = back[which, b * WIDE : (b + 1) * WIDE, :].T
    for i in range(len(landings) + 3):
        whole = stage.at[0, others, :]
        pltpu.make_async_copy(whole, whole, send_sem.at[i]).wait()
    for level, (slots, peers) in enumerate(((one, core_peers), (two, x_peers), (three, y_peers))):
        whole = slots.at[pl.ds(0, len(peers))]
        pltpu.make_async_copy(whole, whole, sum_send.at[level]).wait()


def on_device(queries, keys, values, grad_out, conv_weight, conv_bias, lengths):
    _, frames, width = queries.shape
    seq_len = frames * HEADS
    any_spec = pl.BlockSpec(memory_space=pl.ANY)
    vmem = pl.BlockSpec(memory_space=pltpu.VMEM)
    block = jax.ShapeDtypeStruct(queries.shape, BF16)
    tall = seq_len + 2 * PAD
    query_grad, key_grad, value_grad, weight_grad, bias_grad = pl.pallas_call(
        core,
        out_shape=(
            block,
            block,
            block,
            jax.ShapeDtypeStruct((KERNEL, HEAD), F32),
            jax.ShapeDtypeStruct((1, HEAD), F32),
        ),
        in_specs=[any_spec] * 4 + [vmem, vmem, pl.BlockSpec(memory_space=pltpu.SMEM)],
        out_specs=(vmem,) * 5,
        scratch_shapes=[
            pltpu.VMEM((4, frames, width), BF16),
            pltpu.VMEM((4, width, frames), BF16),
            pltpu.VMEM((WIDE, seq_len), BF16),
            pltpu.VMEM((WIDE, seq_len), BF16),
            pltpu.VMEM((WIDE, seq_len), BF16),
            pltpu.VMEM((WIDE, seq_len), BF16),
            pltpu.VMEM((KERNEL + 1, WIDE), F32),
            pltpu.VMEM((seq_len, seq_len), BF16),
            pltpu.VMEM((tall, WIDE), F32),
            pltpu.VMEM((seq_len, WIDE), F32),
            pltpu.VMEM((seq_len, WIDE), F32),
            pltpu.VMEM((tall, WIDE), F32),
            pltpu.VMEM((seq_len, WIDE), F32),
            pltpu.VMEM((seq_len, WIDE), BF16),
            pltpu.VMEM((WIDE, seq_len), BF16),
            pltpu.VMEM((3, width, frames), BF16),
            pltpu.VMEM((3, width, frames), BF16),
            pltpu.VMEM((KERNEL + 1, 8, WIDE), F32),
            pltpu.VMEM((2, KERNEL + 1, WIDE), F32),
            pltpu.VMEM((4, KERNEL + 1, WIDE), F32),
            pltpu.VMEM((4, KERNEL + 1, WIDE), F32),
            pltpu.SemaphoreType.DMA((4,)),
            pltpu.SemaphoreType.DMA((4,)),
            pltpu.SemaphoreType.DMA((7,)),
            pltpu.SemaphoreType.DMA((7,)),
            pltpu.SemaphoreType.DMA((3,)),
            pltpu.SemaphoreType.DMA((3,)),
        ],
        compiler_params=pltpu.CompilerParams(
            collective_id=0, has_side_effects=True, vmem_limit_bytes=56 << 20
        ),
    )(queries, keys, values, grad_out, conv_weight, conv_bias[None, :], lengths)
    return query_grad, key_grad, value_grad, weight_grad, bias_grad[0]


def solution(mesh):
    return jax.shard_map(
        on_device,
        mesh=mesh,
        in_specs=(
            P("dp", "seq", None),
            P("dp", "seq", None),
            P("dp", "seq", None),
            P("dp", "seq", None),
            P(),
            P(),
            P("dp"),
        ),
        out_specs=(
            P("dp", "seq", None),
            P("dp", "seq", None),
            P("dp", "seq", None),
            P(None, "seq"),
            P("seq"),
        ),
        check_vma=False,
    )
```

time: 793 us -> 116 us (0.15); the launches traced: 779 us -> 116 us
  waiting for transfers between devices: 255 us -> 0 us
  blocking collectives: 180 us -> 0 us
  other arithmetic: 115 us -> 0 us
  Pallas kernels: 0 us -> 108 us
  starting transfers between devices: 102 us -> 0 us
  local copies, waits for them, and re-layouts: 63.7 us -> 6.12 us
  matrix products: 45.2 us -> 0 us
  between operations: 16.5 us -> 1.3 us
    unnamed x2 -> x0, waiting for transfers between devices: 188 us -> none
    psum x1 -> x0, blocking collectives: 133 us -> none  [on_device(): weight_grad, bias_grad = lax.psum((weight_share, bias_share), 'dp')]
    pallas_call x0 -> x1, Pallas kernels: none -> 108 us  [on_device(): pl.pallas_call(core, out_shape=(block, block, block, jax.ShapeDtypeStruct...]
    all_to_all x8 -> x0, starting transfers between devices: 93.2 us -> none  [the longest x1 22.6 us: on_device(): lax.all_to_all(split_heads(attn_grad), 'seq', split_axis=2, concat_axis=1...]
    all_to_all x8 -> x0, waiting for transfers between devices: 58 us -> none  [the longest x1 12.4 us: on_device(): lax.all_to_all(split_heads(attn_grad), 'seq', split_axis=2, concat_axis=1...]
    unnamed x1 -> x0, blocking collectives: 46.9 us -> none
    unnamed x6 -> x0, other arithmetic: 46.6 us -> none
    dot_general x28 -> x0, matrix products: 45.2 us -> none  [the longest x4 14.7 us: block_step(): jnp.einsum('hqk,qhd->khd', probs_low, grad_block, preferred_element_type=...]
  transfers between devices with their start and end apart: 13 -> 0, of which waited for: 10 -> 0; matrix products, arithmetic and copies ran while one was open for 9% -> 0% of each run, Pallas kernels for 0% -> 0%
where the time goes in v1:
time: 116 us
  Pallas kernels  108 us (93%)
  local copies, waits for them, and re-layouts  6.12 us (5%)
  between operations  1.3 us (1%)
    pallas_call x1, Pallas kernels, on_device(): pl.pallas_call(core, out_shape=(block, block, block, jax.ShapeDtypeStruct...  108 us
    unnamed x13, local copies, waits for them, and re-layouts  4.83 us

profile of v1, /device:TPU:1, one launch (start us, length us, event | category | flops | bytes accessed | tf_op | source)
XLA Modules:
  0.0 115.6 jit_solution(3518252782072142859)
XLA Ops:
  1.3 1.3 %broadcast_in_dim.3.bias_ref = f32[1,1536]{1,0:T(1,128)} reshape(f32[1536]{0:T(1024)} %param.12) | data formatting | bytes 12288 | tf_op jit(solution)/shard_map/broadcast_in_dim | solution.py:359
  2.6 108.2 %shard_map.110 = (bf16[1,128,1536]{2,1,0:T(8,128)(2,1)}, bf16[1,128,1536]{2,1,0:T(8,128)(2,1)}, bf16[1,128,1536]{2,1,0:T(8,128)(2,1)}, f32[31,96]{1,0:T(8,128)}, f32[1,96]{1,0:T(1,128)}) custom-call(bf16[1,128,1536]{2,1,0:T(8,128)(2,1)} %q_hbm.1, bf16[1,128,1536]{2,1,0:T(8,128)(2,1)} %k_hbm.1, bf16[1,128,1536]{2,1,0:T(8,128)(2,1)} %v_hbm.1, ...), custom_call_target="tpu_custom_call" | custom-call | tf_op jit(solution)/shard_map/pallas_call | solution.py:316
  110.8 0.0 copy-start.1
  110.8 1.8 %copy.18 = bf16[1,128,1536]{2,1,0:T(8,128)(2,1)} copy(bf16[1,128,1536]{2,1,0:T(8,128)(2,1)} %get-tuple-element.20) | data formatting | bytes 786432
  112.6 0.0 copy-done.1
  112.6 0.0 copy-start
  112.6 0.7 copy.19
  113.4 0.4 copy-done
  113.7 0.0 copy-start.2
  113.7 0.7 copy.20
  114.5 0.0 copy-done.2
  114.5 0.0 copy-start.3
  114.5 0.6 copy.21
  115.1 0.0 copy-done.3
  115.1 0.5 copy.22
Async XLA Ops:
  110.8 1.8 %copy-start.1 = (bf16[1,128,1536]{2,1,0:T(8,128)(2,1)S(1)}, bf16[1,128,1536]{2,1,0:T(8,128)(2,1)}, u32[]{:S(2)}) copy-start(bf16[1,128,1536]{2,1,0:T(8,128)(2,1)} %get-tuple-element.21) | copy-start | bytes 1179652
  112.6 1.1 copy-start
  113.7 0.8 copy-start.2
  114.5 0.6 copy-start.3

commit v2 on v1

v2 whole, which is shorter than its diff:
```python
import math

import jax
import jax.numpy as jnp
from jax import lax
from jax.experimental import pallas as pl
from jax.experimental.pallas import tpu as pltpu
from jax.sharding import PartitionSpec as P

MESH = pl.DeviceIdType.MESH
HEADS = 16
KERNEL = 31
EARLY = False
HEAD = 96
WIDE = 128
PAD = 16
ROWS = 256
CONV = 128
NEG = -1e30
F32 = jnp.float32
BF16 = jnp.bfloat16


def core(
    q_hbm, k_hbm, v_hbm, g_hbm, weight_ref, bias_ref, length_ref,
    dq_ref, dk_ref, dv_ref, dw_ref, db_ref,
    raw, stage, q_t, k_t, v_t, g_t, weights, low, att, out_nat, slope, pre, upper,
    grad_x, grad_t, grad_nat, k_nat, v_nat, stage_out, back, done, tap_sum, one, two, three,
    load_sem, own_sem, send_sem, recv_sem, grad_sem, store_sem, sum_send, sum_recv,
):
    seq_len = q_t.shape[1]
    frames = raw.shape[1]
    width = raw.shape[2]
    me = lax.axis_index("seq")
    dp = lax.axis_index("dp")
    dp_core = lax.rem(dp, 2)
    dp_x = lax.rem(dp // 2, 4)
    dp_y = dp // 8
    length = length_ref[0]

    me_y, me_z = me // 8, lax.rem(me, 8)
    turns = [(dy, dz) for dz in (4, 3, 5, 2, 6, 1, 7, 0) for dy in (1, 0)][:-1]
    seq_peers = [lax.rem(me_y + dy, 2) * 8 + lax.rem(me_z + dz, 8) for dy, dz in turns]
    core_peers = [dp_y * 8 + dp_x * 2 + 1 - dp_core]
    x_peers = [dp_y * 8 + lax.rem(dp_x + s, 4) * 2 + dp_core for s in (1, 2, 3)]
    y_peers = [lax.rem(dp_y + s, 4) * 8 + dp_x * 2 + dp_core for s in (1, 2, 3)]
    barrier = pltpu.get_barrier_semaphore()
    for peer in seq_peers:
        pl.semaphore_signal(barrier, inc=1, device_id={"seq": peer}, device_id_type=MESH)
    for peer in core_peers + x_peers + y_peers:
        pl.semaphore_signal(barrier, inc=1, device_id={"dp": peer}, device_id_type=MESH)

    sources = (k_hbm, q_hbm, v_hbm, g_hbm)
    loads = [
        pltpu.make_async_copy(ref.at[0], raw.at[i], load_sem.at[i])
        for i, ref in enumerate(sources)
    ]
    for load in loads:
        load.start()

    own_lanes = pl.ds(pl.multiple_of(me * frames, frames), frames)
    own_rows = pl.ds(pl.multiple_of(me * HEAD, HEAD), HEAD)
    landings = (k_t, q_t, v_t, g_t)
    others = pl.ds(0, (HEADS - 1) * HEAD)

    early = EARLY

    def turn_around(i):
        loads[i].wait()
        for b in range(width // WIDE):
            stage[i, b * WIDE : (b + 1) * WIDE, :] = raw[i, :, b * WIDE : (b + 1) * WIDE].T

    def send(i):
        target = landings[i].at[pl.ds(0, HEAD), own_lanes]
        for peer in seq_peers:
            pltpu.make_async_remote_copy(
                src_ref=stage.at[i, pl.ds(pl.multiple_of(peer * HEAD, HEAD), HEAD), :],
                dst_ref=target,
                send_sem=send_sem.at[i],
                recv_sem=grad_sem.at[me] if i == 3 else recv_sem.at[i],
                device_id={"seq": peer},
                device_id_type=MESH,
            ).start()
        pltpu.make_async_copy(stage.at[i, own_rows, :], target, own_sem.at[i]).start()

    def sent(i):
        whole = stage.at[0, others, :]
        pltpu.make_async_copy(whole, whole, send_sem.at[i]).wait()

    def arrived(i):
        mine = stage.at[i, own_rows, :]
        pltpu.make_async_copy(mine, mine, own_sem.at[i]).wait()
        whole = landings[i].at[pl.ds(0, HEAD), pl.ds(0, seq_len - frames)]
        pltpu.make_async_copy(whole, whole, recv_sem.at[i]).wait()

    turn_around(0)
    turn_around(1)
    pl.semaphore_wait(barrier, len(seq_peers + core_peers + x_peers + y_peers))
    send(0)
    send(1)
    turn_around(2)
    send(2)
    turn_around(3)
    if not early:
        send(3)

    k_t[HEAD:, :] = jnp.zeros((WIDE - HEAD, seq_len), BF16)
    key_pos = lax.broadcasted_iota(jnp.int32, (16, seq_len), 1)
    key_row = lax.broadcasted_iota(jnp.int32, (16, seq_len), 0)
    mask = jnp.where((key_row == 0) & (key_pos >= length), F32(NEG), F32(0.0))
    k_t[HEAD : HEAD + 16, :] = mask.astype(BF16)
    q_t[HEAD:, :] = jnp.zeros((WIDE - HEAD, seq_len), BF16)
    q_t[HEAD : HEAD + 16, :] = jnp.where(key_row == 0, F32(1.0), F32(0.0)).astype(BF16)
    v_t[HEAD:, :] = jnp.zeros((WIDE - HEAD, seq_len), BF16)
    v_t[HEAD : HEAD + 16, :] = jnp.where(key_row < 3, F32(1.0), F32(0.0)).astype(BF16)
    g_t[HEAD:, :] = jnp.zeros((WIDE - HEAD, seq_len), BF16)
    first = pl.multiple_of((me * HEAD) // WIDE * WIDE, WIDE)
    second = pl.multiple_of(jnp.minimum((me * HEAD) // WIDE + 1, width // WIDE - 1) * WIDE, WIDE)

    def own_columns(ref):
        pair = [ref[..., pl.ds(first, WIDE)], ref[..., pl.ds(second, WIDE)]]
        both = jnp.concatenate([part.reshape(-1, WIDE) for part in pair], axis=1)
        part = both[:, 0:HEAD]
        for turn in range(1, 4):
            at = turn * HEAD % WIDE
            part = jnp.where(lax.rem(me, 4) == turn, both[:, at : at + HEAD], part)
        return part

    weights[...] = jnp.zeros(weights.shape, F32)
    own_taps = own_columns(weight_ref)
    for j in range(KERNEL):
        weights[j, :, 0:HEAD] = jnp.broadcast_to(own_taps[j : j + 1, :], (8, HEAD))
    weights[KERNEL, :, 0:HEAD] = jnp.broadcast_to(own_columns(bias_ref), (8, HEAD))
    zero_rim = jnp.zeros((PAD, WIDE), F32)
    for buffer in (att, pre):
        buffer[0:PAD, :] = zero_rim
        buffer[PAD + seq_len :, :] = zero_rim
    tap_sum[...] = jnp.zeros(tap_sum.shape, F32)

    arrived(0)
    arrived(1)

    rate = F32(math.log2(math.e) / math.sqrt(HEAD))
    steps = seq_len // ROWS

    def weigh(step, _):
        rows = pl.ds(pl.multiple_of(step * ROWS, ROWS), ROWS)
        query = q_t[:, rows].T
        scores = jnp.dot(query, k_t[...], preferred_element_type=F32)
        top = jnp.max(scores, axis=1, keepdims=True)
        low[rows, :] = jnp.exp2((scores - top) * rate).astype(BF16)
        return 0

    def forward(step, _):
        at = pl.multiple_of(step * ROWS, ROWS)
        rows = pl.ds(at, ROWS)
        out = jnp.dot(low[rows, :], v_nat[...], preferred_element_type=F32)
        inverse = 1.0 / out[:, HEAD : HEAD + 1]
        upper[rows, :] = jnp.broadcast_to(inverse, (ROWS, WIDE))
        out = out * inverse
        out_nat[rows, :] = out
        place = at + lax.broadcasted_iota(jnp.int32, (ROWS, WIDE), 0)
        lane = lax.broadcasted_iota(jnp.int32, (ROWS, WIDE), 1)
        shown = jnp.where((place < length) & (lane < HEAD), out, 0.0)
        att[pl.ds(pl.multiple_of(PAD + at, PAD), ROWS), :] = shown.astype(BF16).astype(F32)
        return 0

    def turn(wide_ref, tall_ref):
        for b in range(seq_len // WIDE):
            part = slice(b * WIDE, (b + 1) * WIDE)
            tall_ref[part, :] = wide_ref[:, part].T

    def shifts(buffer, at):
        window = buffer[pl.ds(at, CONV + 2 * PAD), :]
        return [window[r : r + CONV + 2 * PAD - 8, :] for r in range(8)]

    def moved(parts, offset):
        aligned = offset // 8 * 8
        part = parts[offset % 8][aligned : aligned + CONV, :]
        return part.reshape(CONV // 8, 8, WIDE)

    if early:
        sent(0)
        send(3)
    lax.fori_loop(0, steps, weigh, 0)
    turn(k_t, k_nat)
    arrived(2)
    turn(v_t, v_nat)
    lax.fori_loop(0, steps, forward, 0)

    by_shift = sorted(range(1, KERNEL + 1), key=lambda offset: offset % 8)

    def conv(step, _):
        at = pl.multiple_of(step * CONV, CONV)
        parts = shifts(att, at)
        total = jnp.broadcast_to(weights[KERNEL][None], (CONV // 8, 8, WIDE))
        for offset in by_shift:
            total = total + weights[offset - 1][None] * moved(parts, offset)
        total = total.reshape(CONV, WIDE)
        sig = jax.nn.sigmoid(total)
        slope[pl.ds(at, CONV), :] = sig * (1.0 + total * (1.0 - sig))
        return 0

    lax.fori_loop(0, seq_len // CONV, conv, 0)

    def rank(k):
        odd = lax.rem(k, 2)
        z = lax.rem(me_z + 4 + odd * ((k + 1) // 2) - (1 - odd) * (k // 2), 8)
        return z

    def gate(half, z, own=False):
        source = half * 8 + z
        block = stage.at[3, pl.ds(0, HEAD), :]
        pltpu.make_async_copy(block, block, own_sem.at[3] if own else grad_sem.at[source]).wait()
        at = pl.multiple_of(source * CONV, CONV)
        rows = pl.ds(at, CONV)
        grad = g_t[:, rows].T.astype(F32)
        grad_nat[rows, :] = grad
        gated = (grad * slope[rows, :]).astype(BF16).astype(F32)
        pre[pl.ds(pl.multiple_of(PAD + at, PAD), CONV), :] = gated

    def conv_back(step, _):
        at = pl.multiple_of(step * CONV, CONV)
        rows = pl.ds(at, CONV)
        parts = shifts(pre, at)
        total = grad_nat[rows, :].reshape(CONV // 8, 8, WIDE)
        for offset in by_shift:
            total = total + weights[KERNEL - offset][None] * moved(parts, offset)
        total = total.reshape(CONV, WIDE)
        place = at + lax.broadcasted_iota(jnp.int32, (CONV, WIDE), 0)
        lane = lax.broadcasted_iota(jnp.int32, (CONV, WIDE), 1)
        total = jnp.where((place < length) & (lane < HEAD), total, 0.0).astype(BF16).astype(F32)
        scaled = (total * upper[rows, :]).astype(BF16).astype(F32)
        delta = -jnp.sum(scaled * out_nat[rows, :], axis=1, keepdims=True)
        high = delta.astype(BF16).astype(F32)
        middle = (delta - high).astype(BF16).astype(F32)
        last = delta - high - middle
        scaled = jnp.where(lane == HEAD, high, scaled)
        scaled = jnp.where(lane == HEAD + 1, middle, scaled)
        scaled = jnp.where(lane == HEAD + 2, last, scaled).astype(BF16)
        grad_x[rows, :] = scaled
        grad_t[:, rows] = scaled.T
        return 0

    def gate_both(k, _):
        gate(1 - me_y, rank(k))
        gate(me_y, rank(k))
        return 0

    def back_both(k, _):
        for half in (0, 1):
            conv_back(half * 8 + rank(k), 0)
        return 0

    def gate_and_back(k, _):
        gate_both(k, 0)
        return back_both(k - 2, 0)

    lax.fori_loop(0, 2, gate_both, 0)
    lax.fori_loop(2, 7, gate_and_back, 0)
    gate(1 - me_y, me_z)
    gate(me_y, me_z, own=True)
    lax.fori_loop(5, 8, back_both, 0)

    out_sent = [len(landings) + i for i in range(3)]

    def send_back(which, step):
        for part in range(ROWS // frames):
            peer = step * (ROWS // frames) + part
            source = stage_out.at[which, pl.ds(pl.multiple_of(peer * HEAD, HEAD), HEAD), :]
            target = back.at[which, own_rows, :]

            @pl.when(peer != me)
            def _():
                pltpu.make_async_remote_copy(
                    src_ref=source,
                    dst_ref=target,
                    send_sem=send_sem.at[out_sent[which]],
                    recv_sem=recv_sem.at[out_sent[which]],
                    device_id={"seq": peer},
                    device_id_type=MESH,
                ).start()

    def put(which, step, block):
        for part in range(ROWS // frames):
            peer = step * (ROWS // frames) + part
            piece = block[:, part * frames : (part + 1) * frames]
            stage_out[which, pl.ds(pl.multiple_of(peer * HEAD, HEAD), HEAD), :] = piece
        send_back(which, step)


    def far_first(step):
        k = step // 2
        odd = lax.rem(k, 2)
        pair = lax.rem(me_z // 2 + 2 + (1 - odd) * (k // 2) - odd * ((k + 1) // 2) + 4, 4)
        return lax.rem(me_y + 1 + lax.rem(step, 2), 2) * 4 + pair

    def value_step(step, _):
        step = far_first(step)
        columns = pl.ds(pl.multiple_of(step * ROWS, ROWS), ROWS)
        block = jnp.dot(grad_t[0:HEAD, :], low[:, columns], preferred_element_type=F32)
        put(2, step, block.astype(BF16))
        return 0

    lax.fori_loop(0, steps, value_step, 0)

    def taps(step, _):
        at = pl.multiple_of(step * CONV, CONV)
        parts = shifts(att, at)
        gated = pre[pl.ds(pl.multiple_of(PAD + at, PAD), CONV), :].reshape(CONV // 8, 8, WIDE)
        for offset in by_shift:
            tap_sum[offset - 1] += jnp.sum(gated * moved(parts, offset), axis=0)
        tap_sum[KERNEL] += jnp.sum(gated, axis=0)
        return 0

    lax.fori_loop(0, seq_len // CONV, taps, 0)

    def sum_start(level, slots, mine, peers, value):
        slots[mine] = value
        for peer in peers:
            pltpu.make_async_remote_copy(
                src_ref=slots.at[mine],
                dst_ref=slots.at[mine],
                send_sem=sum_send.at[level],
                recv_sem=sum_recv.at[level],
                device_id={"dp": peer},
                device_id_type=MESH,
            ).start()

    def sum_end(level, slots, peers):
        whole = slots.at[pl.ds(0, len(peers))]
        pltpu.make_async_copy(whole, whole, sum_recv.at[level]).wait()
        value = slots[0]
        for i in range(1, len(peers) + 1):
            value = value + slots[i]
        return value

    sum_start(0, one, dp_core, core_peers, jnp.sum(tap_sum[...], axis=1))

    back_scale = F32(1.0 / math.sqrt(HEAD))

    def query_step(step, _):
        step = far_first(step)
        rows = pl.ds(pl.multiple_of(step * ROWS, ROWS), ROWS)
        change = jnp.dot(grad_x[rows, :], v_t[...], preferred_element_type=F32)
        diff = (change * low[rows, :].astype(F32)).astype(BF16)
        low[rows, :] = diff
        block = jnp.dot(diff, k_nat[...], preferred_element_type=F32)
        put(0, step, (block * back_scale).astype(BF16).T[0:HEAD, :])
        return 0

    lax.fori_loop(0, steps, query_step, 0)
    sum_start(1, two, dp_x, x_peers, sum_end(0, one, core_peers))

    def key_step(step, _):
        step = far_first(step)
        columns = pl.ds(pl.multiple_of(step * ROWS, ROWS), ROWS)
        block = jnp.dot(q_t[0:HEAD, :], low[:, columns], preferred_element_type=F32)
        put(1, step, (block * back_scale).astype(BF16))
        return 0

    lax.fori_loop(0, steps, key_step, 0)
    sum_start(2, three, dp_y, y_peers, sum_end(1, two, x_peers))
    sums = sum_end(2, three, y_peers)
    dw_ref[...] = sums[0:KERNEL, 0:HEAD]
    db_ref[...] = sums[KERNEL : KERNEL + 1, 0:HEAD]

    stores = []
    for which, result in ((2, dv_ref), (0, dq_ref), (1, dk_ref)):
        back[which, own_rows, :] = stage_out[which, own_rows, :]
        whole = back.at[which, others, :]
        pltpu.make_async_copy(whole, whole, recv_sem.at[out_sent[which]]).wait()
        for b in range(width // WIDE):
            done[which, :, b * WIDE : (b + 1) * WIDE] = back[which, b * WIDE : (b + 1) * WIDE, :].T
        store = pltpu.make_async_copy(done.at[which], result.at[0], store_sem.at[which])
        store.start()
        stores.append(store)
    for store in stores:
        store.wait()
    for i in range(1 if early else 0, len(landings) + 3):
        sent(i)
    for level, (slots, peers) in enumerate(((one, core_peers), (two, x_peers), (three, y_peers))):
        whole = slots.at[pl.ds(0, len(peers))]
        pltpu.make_async_copy(whole, whole, sum_send.at[level]).wait()


def hand_over(*refs):
    sems = refs[-1]
    copies = [pltpu.make_async_copy(refs[i], refs[5 + i], sems.at[i]) for i in range(5)]
    for copy in copies:
        copy.start()
    for copy in copies:
        copy.wait()


def on_device(queries, keys, values, grad_out, conv_weight, conv_bias, lengths):
    _, frames, width = queries.shape
    seq_len = frames * HEADS
    any_spec = pl.BlockSpec(memory_space=pl.ANY)
    vmem = pl.BlockSpec(memory_space=pltpu.VMEM)
    block = jax.ShapeDtypeStruct(queries.shape, BF16)
    tall = seq_len + 2 * PAD
    query_grad, key_grad, value_grad, weight_grad, bias_grad = pl.pallas_call(
        core,
        out_shape=(
            block,
            block,
            block,
            jax.ShapeDtypeStruct((KERNEL, HEAD), F32),
            jax.ShapeDtypeStruct((1, HEAD), F32),
        ),
        in_specs=[any_spec] * 4 + [vmem, vmem, pl.BlockSpec(memory_space=pltpu.SMEM)],
        out_specs=(any_spec,) * 3 + (vmem,) * 2,
        scratch_shapes=[
            pltpu.VMEM((4, frames, width), BF16),
            pltpu.VMEM((4, width, frames), BF16),
            pltpu.VMEM((WIDE, seq_len), BF16),
            pltpu.VMEM((WIDE, seq_len), BF16),
            pltpu.VMEM((WIDE, seq_len), BF16),
            pltpu.VMEM((WIDE, seq_len), BF16),
            pltpu.VMEM((KERNEL + 1, 8, WIDE), F32),
            pltpu.VMEM((seq_len, seq_len), BF16),
            pltpu.VMEM((tall, WIDE), F32),
            pltpu.VMEM((seq_len, WIDE), F32),
            pltpu.VMEM((seq_len, WIDE), F32),
            pltpu.VMEM((tall, WIDE), F32),
            pltpu.VMEM((seq_len, WIDE), F32),
            pltpu.VMEM((seq_len, WIDE), BF16),
            pltpu.VMEM((WIDE, seq_len), BF16),
            pltpu.VMEM((seq_len, WIDE), F32),
            pltpu.VMEM((seq_len, WIDE), BF16),
            pltpu.VMEM((seq_len, WIDE), BF16),
            pltpu.VMEM((3, width, frames), BF16),
            pltpu.VMEM((3, width, frames), BF16),
            pltpu.VMEM((3, frames, width), BF16),
            pltpu.VMEM((KERNEL + 1, 8, WIDE), F32),
            pltpu.VMEM((2, KERNEL + 1, WIDE), F32),
            pltpu.VMEM((4, KERNEL + 1, WIDE), F32),
            pltpu.VMEM((4, KERNEL + 1, WIDE), F32),
            pltpu.SemaphoreType.DMA((4,)),
            pltpu.SemaphoreType.DMA((4,)),
            pltpu.SemaphoreType.DMA((7,)),
            pltpu.SemaphoreType.DMA((7,)),
            pltpu.SemaphoreType.DMA((HEADS,)),
            pltpu.SemaphoreType.DMA((3,)),
            pltpu.SemaphoreType.DMA((3,)),
            pltpu.SemaphoreType.DMA((3,)),
        ],
        compiler_params=pltpu.CompilerParams(
            collective_id=0, has_side_effects=True, vmem_limit_bytes=56 << 20
        ),
    )(queries, keys, values, grad_out, conv_weight, conv_bias, lengths)
    found = (query_grad, key_grad, value_grad, weight_grad, bias_grad)
    found = pl.pallas_call(
        hand_over,
        out_shape=tuple(jax.ShapeDtypeStruct(part.shape, part.dtype) for part in found),
        in_specs=[vmem] * 5,
        out_specs=(any_spec,) * 5,
        scratch_shapes=[pltpu.SemaphoreType.DMA((5,))],
    )(*found)
    return *found[:4], found[4][0]


def solution(mesh):
    return jax.shard_map(
        on_device,
        mesh=mesh,
        in_specs=(
            P("dp", "seq", None),
            P("dp", "seq", None),
            P("dp", "seq", None),
            P("dp", "seq", None),
            P(),
            P(),
            P("dp"),
        ),
        out_specs=(
            P("dp", "seq", None),
            P("dp", "seq", None),
            P("dp", "seq", None),
            P(None, "seq"),
            P("seq"),
        ),
        check_vma=False,
    )
```

time: 116 us -> 99.1 us (0.85)
  Pallas kernels: 108 us -> 97.7 us
  local copies, waits for them, and re-layouts: 6.12 us -> 0 us
    pallas_call x1, Pallas kernels: 108 us -> 95.4 us  [on_device(): pl.pallas_call(core, out_shape=(block, block, block, jax.ShapeDtypeStruct...]
    unnamed x13 -> x0, local copies, waits for them, and re-layouts: 4.83 us -> none
    pallas_call x0 -> x1, Pallas kernels: none -> 2.31 us  [on_device(): pl.pallas_call(hand_over, out_shape=tuple((jax.ShapeDtypeStruct(part.shap...]
    broadcast_in_dim x1 -> x0, local copies, waits for them, and re-layouts: 1.3 us -> none  [on_device(): conv_bias[None, :]]
where the time goes in v2:
time: 99.1 us; the launch traced here: 98.9 us
  Pallas kernels  97.7 us (99%)
  between operations  1.29 us (1%)
    pallas_call x1, Pallas kernels, on_device(): pl.pallas_call(core, out_shape=(block, block, block, jax.ShapeDtypeStruct...  95.4 us
    pallas_call x1, Pallas kernels, on_device(): pl.pallas_call(hand_over, out_shape=tuple((jax.ShapeDtypeStruct(part.shap...  2.31 us

profile of v2, /device:TPU:1, one launch (start us, length us, event | category | flops | bytes accessed | tf_op | source)
XLA Modules:
  0.0 98.9 jit_solution(9505521173978997523)
XLA Ops:
  1.3 95.4 %shard_map.110 = (bf16[1,128,1536]{2,1,0:T(8,128)(2,1)}, bf16[1,128,1536]{2,1,0:T(8,128)(2,1)}, bf16[1,128,1536]{2,1,0:T(8,128)(2,1)}, f32[31,96]{1,0:T(8,128)}, f32[1,96]{1,0:T(1,128)}) custom-call(bf16[1,128,1536]{2,1,0:T(8,128)(2,1)} %q_hbm.1, bf16[1,128,1536]{2,1,0:T(8,128)(2,1)} %k_hbm.1, bf16[1,128,1536]{2,1,0:T(8,128)(2,1)} %v_hbm.1, ...), custom_call_target="tpu_custom_call" | custom-call | tf_op jit(solution)/shard_map/pallas_call | solution.py:403
  96.6 2.3 %shard_map.111 = (bf16[1,128,1536]{2,1,0:T(8,128)(2,1)}, bf16[1,128,1536]{2,1,0:T(8,128)(2,1)}, bf16[1,128,1536]{2,1,0:T(8,128)(2,1)}, f32[31,96]{1,0:T(8,128)}, f32[1,96]{1,0:T(1,128)}) custom-call(bf16[1,128,1536]{2,1,0:T(8,128)(2,1)} %get-tuple-element.15.refs_0_, bf16[1,128,1536]{2,1,0:T(8,128)(2,1)} %get-tuple-element.16.refs_1_, ...), custom_call_target="tpu_custom_call" | custom-call | tf_op jit(solution)/shard_map/pallas_call | solution.py:454

commit v3 on v2

--- a/solution.py
+++ b/solution.py
@@ -25,8 +25,8 @@
     q_hbm, k_hbm, v_hbm, g_hbm, weight_ref, bias_ref, length_ref,
     dq_ref, dk_ref, dv_ref, dw_ref, db_ref,
     raw, stage, q_t, k_t, v_t, g_t, weights, low, att, out_nat, slope, pre, upper,
-    grad_x, grad_t, grad_nat, k_nat, v_nat, stage_out, back, done, tap_sum, one, two, three,
-    load_sem, own_sem, send_sem, recv_sem, grad_sem, store_sem, sum_send, sum_recv,
+    grad_x, grad_t, grad_nat, k_nat, diffs, stage_out, back, done, tap_sum, one, two, three,
+    load_sem, own_sem, send_sem, recv_sem, block_sem, store_sem, sum_send, sum_recv,
 ):
     seq_len = q_t.shape[1]
     frames = raw.shape[1]
@@ -51,12 +51,15 @@
         pl.semaphore_signal(barrier, inc=1, device_id={"dp": peer}, device_id_type=MESH)
 
     sources = (k_hbm, q_hbm, v_hbm, g_hbm)
-    loads = [
-        pltpu.make_async_copy(ref.at[0], raw.at[i], load_sem.at[i])
-        for i, ref in enumerate(sources)
-    ]
-    for load in loads:
-        load.start()
+    quarter = width // 4
+    loads = {}
+    for i, ref in enumerate(sources):
+        for c in range(4):
+            part = pl.ds(c * quarter, quarter)
+            loads[i, c] = pltpu.make_async_copy(
+                ref.at[0, :, part], raw.at[i, :, part], load_sem.at[i, c]
+            )
+            loads[i, c].start()
 
     own_lanes = pl.ds(pl.multiple_of(me * frames, frames), frames)
     own_rows = pl.ds(pl.multiple_of(me * HEAD, HEAD), HEAD)
@@ -66,8 +69,9 @@
     early = EARLY
 
     def turn_around(i):
-        loads[i].wait()
         for b in range(width // WIDE):
+            if b * WIDE % quarter == 0:
+                loads[i, b * WIDE // quarter].wait()
             stage[i, b * WIDE : (b + 1) * WIDE, :] = raw[i, :, b * WIDE : (b + 1) * WIDE].T
 
     def send(i):
@@ -77,7 +81,7 @@
                 src_ref=stage.at[i, pl.ds(pl.multiple_of(peer * HEAD, HEAD), HEAD), :],
                 dst_ref=target,
                 send_sem=send_sem.at[i],
-                recv_sem=grad_sem.at[me] if i == 3 else recv_sem.at[i],
+                recv_sem=block_sem.at[i - 1, me] if i else recv_sem.at[i],
                 device_id={"seq": peer},
                 device_id_type=MESH,
             ).start()
@@ -86,6 +90,28 @@
     def sent(i):
         whole = stage.at[0, others, :]
         pltpu.make_async_copy(whole, whole, send_sem.at[i]).wait()
+
+    def rank(k):
+        odd = lax.rem(k, 2)
+        z = lax.rem(me_z + 4 + odd * ((k + 1) // 2) - (1 - odd) * (k // 2), 8)
+        return z
+
+    def spots_of(k):
+        return [half * 8 + rank(k) for half in (1 - me_y, me_y)]
+
+    def rows_of(spots):
+        return [pl.ds(pl.multiple_of(spot * CONV, CONV), CONV) for spot in spots]
+
+    def landed(i, spot, own=False):
+        block = stage.at[i, pl.ds(0, HEAD), :]
+        sem = own_sem.at[i] if own else block_sem.at[i - 1, spot]
+        pltpu.make_async_copy(block, block, sem).wait()
+
+    def landed_pair(i, k, own):
+        spots = spots_of(k)
+        landed(i, spots[0])
+        landed(i, spots[1], own)
+        return rows_of(spots)
 
     def arrived(i):
         mine = stage.at[i, own_rows, :]
@@ -136,25 +162,43 @@
         buffer[0:PAD, :] = zero_rim
         buffer[PAD + seq_len :, :] = zero_rim
     tap_sum[...] = jnp.zeros(tap_sum.shape, F32)
+    out_nat[...] = jnp.zeros(out_nat.shape, F32)
+
+    if early:
+        sent(0)
+        send(3)
+    def turn(wide_ref, tall_ref):
+        for b in range(seq_len // WIDE):
+            part = slice(b * WIDE, (b + 1) * WIDE)
+            tall_ref[part, :] = wide_ref[:, part].T
 
     arrived(0)
-    arrived(1)
+    turn(k_t, k_nat)
 
     rate = F32(math.log2(math.e) / math.sqrt(HEAD))
     steps = seq_len // ROWS
 
-    def weigh(step, _):
-        rows = pl.ds(pl.multiple_of(step * ROWS, ROWS), ROWS)
-        query = q_t[:, rows].T
+    def weigh(k, _, own=False):
+        rows = landed_pair(1, k, own)
+        query = jnp.concatenate([q_t[:, part] for part in rows], axis=1).T
         scores = jnp.dot(query, k_t[...], preferred_element_type=F32)
         top = jnp.max(scores, axis=1, keepdims=True)
-        low[rows, :] = jnp.exp2((scores - top) * rate).astype(BF16)
+        exped = jnp.exp2((scores - top) * rate).astype(BF16)
+        for i in range(2):
+            low[rows[i], :] = exped[i * CONV : (i + 1) * CONV, :]
+        return 0
+
+    def attend(k, _, own=False):
+        rows = landed_pair(2, k, own)
+        value = jnp.concatenate([v_t[:, part] for part in rows], axis=1).T
+        exped = jnp.concatenate([low[:, part] for part in rows], axis=1)
+        out_nat[...] += jnp.dot(exped, value, preferred_element_type=F32)
         return 0
 
     def forward(step, _):
         at = pl.multiple_of(step * ROWS, ROWS)
         rows = pl.ds(at, ROWS)
-        out = jnp.dot(low[rows, :], v_nat[...], preferred_element_type=F32)
+        out = out_nat[rows, :]
         inverse = 1.0 / out[:, HEAD : HEAD + 1]
         upper[rows, :] = jnp.broadcast_to(inverse, (ROWS, WIDE))
         out = out * inverse
@@ -165,11 +209,6 @@
         att[pl.ds(pl.multiple_of(PAD + at, PAD), ROWS), :] = shown.astype(BF16).astype(F32)
         return 0
 
-    def turn(wide_ref, tall_ref):
-        for b in range(seq_len // WIDE):
-            part = slice(b * WIDE, (b + 1) * WIDE)
-            tall_ref[part, :] = wide_ref[:, part].T
-
     def shifts(buffer, at):
         window = buffer[pl.ds(at, CONV + 2 * PAD), :]
         return [window[r : r + CONV + 2 * PAD - 8, :] for r in range(8)]
@@ -179,15 +218,10 @@
         part = parts[offset % 8][aligned : aligned + CONV, :]
         return part.reshape(CONV // 8, 8, WIDE)
 
-    if early:
-        sent(0)
-        send(3)
-    lax.fori_loop(0, steps, weigh, 0)
-    turn(k_t, k_nat)
-    arrived(2)
-    turn(v_t, v_nat)
-    lax.fori_loop(0, steps, forward, 0)
-
+    lax.fori_loop(0, 7, weigh, 0)
+    weigh(7, 0, own=True)
+    lax.fori_loop(0, 7, attend, 0)
+    attend(7, 0, own=True)
     by_shift = sorted(range(1, KERNEL + 1), key=lambda offset: offset % 8)
 
     def conv(step, _):
@@ -201,17 +235,20 @@
         slope[pl.ds(at, CONV), :] = sig * (1.0 + total * (1.0 - sig))
         return 0
 
-    lax.fori_loop(0, seq_len // CONV, conv, 0)
-
-    def rank(k):
-        odd = lax.rem(k, 2)
-        z = lax.rem(me_z + 4 + odd * ((k + 1) // 2) - (1 - odd) * (k // 2), 8)
-        return z
+    def conv_and_forward(step, _):
+        conv(2 * step - 3, 0)
+        conv(2 * step - 2, 0)
+        return forward(step, 0)
+
+    forward(0, 0)
+    conv(0, 0)
+    forward(1, 0)
+    lax.fori_loop(2, steps, conv_and_forward, 0)
+    lax.fori_loop(2 * steps - 3, 2 * steps, conv, 0)
 
     def gate(half, z, own=False):
         source = half * 8 + z
-        block = stage.at[3, pl.ds(0, HEAD), :]
-        pltpu.make_async_copy(block, block, own_sem.at[3] if own else grad_sem.at[source]).wait()
+        landed(3, source, own)
         at = pl.multiple_of(source * CONV, CONV)
         rows = pl.ds(at, CONV)
         grad = g_t[:, rows].T.astype(F32)
@@ -242,44 +279,75 @@
         grad_t[:, rows] = scaled.T
         return 0
 
+    out_sent = [len(landings) + i for i in range(3)]
+
+    def send_one(which, peer):
+        pltpu.make_async_remote_copy(
+            src_ref=stage_out.at[which, pl.ds(pl.multiple_of(peer * HEAD, HEAD), HEAD), :],
+            dst_ref=back.at[which, own_rows, :],
+            send_sem=send_sem.at[out_sent[which]],
+            recv_sem=recv_sem.at[out_sent[which]],
+            device_id={"seq": peer},
+            device_id_type=MESH,
+        ).start()
+
+    back_scale = F32(1.0 / math.sqrt(HEAD))
+
+    def query_both(k):
+        spots = spots_of(k)
+        rows = rows_of(spots)
+        grads = jnp.concatenate([grad_x[part, :] for part in rows], axis=0)
+        change = jnp.dot(grads, v_t[...], preferred_element_type=F32)
+        exped = jnp.concatenate([low[part, :] for part in rows], axis=0).astype(F32)
+        diff = (change * exped).astype(BF16)
+        block = jnp.dot(diff, k_nat[...], preferred_element_type=F32)
+        block = (block * back_scale).astype(BF16).T[0:HEAD, :]
+        for i in range(2):
+            diffs[rows[i], :] = diff[i * CONV : (i + 1) * CONV, :]
+            place = pl.ds(pl.multiple_of(spots[i] * HEAD, HEAD), HEAD)
+            stage_out[0, place, :] = block[:, i * CONV : (i + 1) * CONV]
+        return spots
+
     def gate_both(k, _):
         gate(1 - me_y, rank(k))
         gate(me_y, rank(k))
         return 0
 
-    def back_both(k, _):
-        for half in (0, 1):
+    def back_both(k):
+        for half in (1 - me_y, me_y):
             conv_back(half * 8 + rank(k), 0)
-        return 0
-
-    def gate_and_back(k, _):
+
+    def flow(k, _):
         gate_both(k, 0)
-        return back_both(k - 2, 0)
-
-    lax.fori_loop(0, 2, gate_both, 0)
-    lax.fori_loop(2, 7, gate_and_back, 0)
+        for spot in query_and_back(k):
+            send_one(0, spot)
+        return 0
+
+    def query_and_back(k):
+        spots = query_both(k - 3)
+        back_both(k - 2)
+        return spots
+
+    def flow_end(k, _):
+        for spot in query_and_back(k):
+            send_one(0, spot)
+        return 0
+
+    lax.fori_loop(0, 3, gate_both, 0)
+    back_both(0)
+    lax.fori_loop(3, 7, flow, 0)
     gate(1 - me_y, me_z)
     gate(me_y, me_z, own=True)
-    lax.fori_loop(5, 8, back_both, 0)
-
-    out_sent = [len(landings) + i for i in range(3)]
+    lax.fori_loop(7, 10, flow_end, 0)
+    send_one(0, query_both(7)[0])
 
     def send_back(which, step):
         for part in range(ROWS // frames):
             peer = step * (ROWS // frames) + part
-            source = stage_out.at[which, pl.ds(pl.multiple_of(peer * HEAD, HEAD), HEAD), :]
-            target = back.at[which, own_rows, :]
 
             @pl.when(peer != me)
             def _():
-                pltpu.make_async_remote_copy(
-                    src_ref=source,
-                    dst_ref=target,
-                    send_sem=send_sem.at[out_sent[which]],
-                    recv_sem=recv_sem.at[out_sent[which]],
-                    device_id={"seq": peer},
-                    device_id_type=MESH,
-                ).start()
+                send_one(which, peer)
 
     def put(which, step, block):
         for part in range(ROWS // frames):
@@ -337,44 +405,41 @@
 
     sum_start(0, one, dp_core, core_peers, jnp.sum(tap_sum[...], axis=1))
 
-    back_scale = F32(1.0 / math.sqrt(HEAD))
-
-    def query_step(step, _):
-        step = far_first(step)
-        rows = pl.ds(pl.multiple_of(step * ROWS, ROWS), ROWS)
-        change = jnp.dot(grad_x[rows, :], v_t[...], preferred_element_type=F32)
-        diff = (change * low[rows, :].astype(F32)).astype(BF16)
-        low[rows, :] = diff
-        block = jnp.dot(diff, k_nat[...], preferred_element_type=F32)
-        put(0, step, (block * back_scale).astype(BF16).T[0:HEAD, :])
-        return 0
-
-    lax.fori_loop(0, steps, query_step, 0)
-    sum_start(1, two, dp_x, x_peers, sum_end(0, one, core_peers))
 
     def key_step(step, _):
         step = far_first(step)
         columns = pl.ds(pl.multiple_of(step * ROWS, ROWS), ROWS)
-        block = jnp.dot(q_t[0:HEAD, :], low[:, columns], preferred_element_type=F32)
+        block = jnp.dot(q_t[0:HEAD, :], diffs[:, columns], preferred_element_type=F32)
         put(1, step, (block * back_scale).astype(BF16))
         return 0
 
     lax.fori_loop(0, steps, key_step, 0)
-    sum_start(2, three, dp_y, y_peers, sum_end(1, two, x_peers))
-    sums = sum_end(2, three, y_peers)
-    dw_ref[...] = sums[0:KERNEL, 0:HEAD]
-    db_ref[...] = sums[KERNEL : KERNEL + 1, 0:HEAD]
+    sum_start(1, two, dp_x, x_peers, sum_end(0, one, core_peers))
 
     stores = []
-    for which, result in ((2, dv_ref), (0, dq_ref), (1, dk_ref)):
+
+    def collect(which, result):
         back[which, own_rows, :] = stage_out[which, own_rows, :]
         whole = back.at[which, others, :]
         pltpu.make_async_copy(whole, whole, recv_sem.at[out_sent[which]]).wait()
         for b in range(width // WIDE):
             done[which, :, b * WIDE : (b + 1) * WIDE] = back[which, b * WIDE : (b + 1) * WIDE, :].T
-        store = pltpu.make_async_copy(done.at[which], result.at[0], store_sem.at[which])
-        store.start()
-        stores.append(store)
+            if (b + 1) * WIDE % quarter == 0:
+                c = b * WIDE // quarter
+                part = pl.ds(c * quarter, quarter)
+                store = pltpu.make_async_copy(
+                    done.at[which, :, part], result.at[0, :, part], store_sem.at[which, c]
+                )
+                store.start()
+                stores.append(store)
+
+    collect(0, dq_ref)
+    sum_start(2, three, dp_y, y_peers, sum_end(1, two, x_peers))
+    collect(2, dv_ref)
+    sums = sum_end(2, three, y_peers)
+    dw_ref[...] = sums[0:KERNEL, 0:HEAD]
+    db_ref[...] = sums[KERNEL : KERNEL + 1, 0:HEAD]
+    collect(1, dk_ref)
     for store in stores:
         store.wait()
     for i in range(1 if early else 0, len(landings) + 3):
@@ -385,12 +450,33 @@
 
 
 def hand_over(*refs):
-    sems = refs[-1]
-    copies = [pltpu.make_async_copy(refs[i], refs[5 + i], sems.at[i]) for i in range(5)]
-    for copy in copies:
-        copy.start()
-    for copy in copies:
-        copy.wait()
+    given, results, held, small, bias, in_sem, out_sem = refs[:5], refs[5:10], *refs[10:]
+    quarter = held.shape[2] // 4
+    copies = []
+    for i in range(3):
+        for c in range(4):
+            part = pl.ds(c * quarter, quarter)
+            where = held.at[i, :, part]
+            copies.append(
+                (
+                    pltpu.make_async_copy(given[i].at[0, :, part], where, in_sem.at[4 * i + c]),
+                    pltpu.make_async_copy(where, results[i].at[0, :, part], out_sem.at[4 * i + c]),
+                )
+            )
+    for i, where in ((3, small), (4, bias)):
+        copies.append(
+            (
+                pltpu.make_async_copy(given[i], where, in_sem.at[9 + i]),
+                pltpu.make_async_copy(where, results[i], out_sem.at[9 + i]),
+            )
+        )
+    for fetch, _ in copies:
+        fetch.start()
+    for fetch, put in copies:
+        fetch.wait()
+        put.start()
+    for _, put in copies:
+        put.wait()
 
 
 def on_device(queries, keys, values, grad_out, conv_weight, conv_bias, lengths):
@@ -429,7 +515,7 @@
             pltpu.VMEM((WIDE, seq_len), BF16),
             pltpu.VMEM((seq_len, WIDE), F32),
             pltpu.VMEM((seq_len, WIDE), BF16),
-            pltpu.VMEM((seq_len, WIDE), BF16),
+            pltpu.VMEM((seq_len, seq_len), BF16),
             pltpu.VMEM((3, width, frames), BF16),
             pltpu.VMEM((3, width, frames), BF16),
             pltpu.VMEM((3, frames, width), BF16),
@@ -437,12 +523,12 @@
             pltpu.VMEM((2, KERNEL + 1, WIDE), F32),
             pltpu.VMEM((4, KERNEL + 1, WIDE), F32),
             pltpu.VMEM((4, KERNEL + 1, WIDE), F32),
-            pltpu.SemaphoreType.DMA((4,)),
+            pltpu.SemaphoreType.DMA((4, 4)),
             pltpu.SemaphoreType.DMA((4,)),
             pltpu.SemaphoreType.DMA((7,)),
             pltpu.SemaphoreType.DMA((7,)),
-            pltpu.SemaphoreType.DMA((HEADS,)),
-            pltpu.SemaphoreType.DMA((3,)),
+            pltpu.SemaphoreType.DMA((3, HEADS)),
+            pltpu.SemaphoreType.DMA((3, 4)),
             pltpu.SemaphoreType.DMA((3,)),
             pltpu.SemaphoreType.DMA((3,)),
         ],
@@ -454,9 +540,16 @@
     found = pl.pallas_call(
         hand_over,
         out_shape=tuple(jax.ShapeDtypeStruct(part.shape, part.dtype) for part in found),
-        in_specs=[vmem] * 5,
+        in_specs=[any_spec] * 5,
         out_specs=(any_spec,) * 5,
-        scratch_shapes=[pltpu.SemaphoreType.DMA((5,))],
+        scratch_shapes=[
+            pltpu.VMEM((3, frames, width), BF16),
+            pltpu.VMEM((KERNEL, HEAD), F32),
+            pltpu.VMEM((1, HEAD), F32),
+            pltpu.SemaphoreType.DMA((14,)),
+            pltpu.SemaphoreType.DMA((14,)),
+        ],
+        compiler_params=pltpu.CompilerParams(vmem_limit_bytes=56 << 20),
     )(*found)
     return *found[:4], found[4][0]
 

time: 99.1 us -> 94.5 us (0.954)
  Pallas kernels: 97.7 us -> 92.8 us
    pallas_call x1, Pallas kernels: 95.4 us -> 90.6 us  [on_device(): pl.pallas_call(core, out_shape=(block, block, block, jax.ShapeDtypeStruct...]
where the time goes in v3:
time: 94.5 us; the launch traced here: 94.1 us
  Pallas kernels  92.8 us (98%)
  between operations  1.29 us (1%)
    pallas_call x1, Pallas kernels, on_device(): pl.pallas_call(core, out_shape=(block, block, block, jax.ShapeDtypeStruct...  90.6 us
    pallas_call x1, Pallas kernels, on_device(): pl.pallas_call(hand_over, out_shape=tuple((jax.ShapeDtypeStruct(part.shap...  2.24 us

profile of v3, /device:TPU:1, one launch (start us, length us, event | category | flops | bytes accessed | tf_op | source)
XLA Modules:
  0.0 94.1 jit_solution(11065826111350174446)
XLA Ops:
  1.3 90.6 %shard_map.110 = (bf16[1,128,1536]{2,1,0:T(8,128)(2,1)}, bf16[1,128,1536]{2,1,0:T(8,128)(2,1)}, bf16[1,128,1536]{2,1,0:T(8,128)(2,1)}, f32[31,96]{1,0:T(8,128)}, f32[1,96]{1,0:T(1,128)}) custom-call(bf16[1,128,1536]{2,1,0:T(8,128)(2,1)} %q_hbm.1, bf16[1,128,1536]{2,1,0:T(8,128)(2,1)} %k_hbm.1, bf16[1,128,1536]{2,1,0:T(8,128)(2,1)} %v_hbm.1, ...), custom_call_target="tpu_custom_call" | custom-call | tf_op jit(solution)/shard_map/pallas_call | solution.py:489
  91.9 2.2 %shard_map.111 = (bf16[1,128,1536]{2,1,0:T(8,128)(2,1)}, bf16[1,128,1536]{2,1,0:T(8,128)(2,1)}, bf16[1,128,1536]{2,1,0:T(8,128)(2,1)}, f32[31,96]{1,0:T(8,128)}, f32[1,96]{1,0:T(1,128)}) custom-call(bf16[1,128,1536]{2,1,0:T(8,128)(2,1)} %get-tuple-element.15.refs_0_, bf16[1,128,1536]{2,1,0:T(8,128)(2,1)} %get-tuple-element.16.refs_1_, ...), custom_call_target="tpu_custom_call" | custom-call | tf_op jit(solution)/shard_map/pallas_call | solution.py:540

commit v4 on v3

--- a/solution.py
+++ b/solution.py
@@ -25,8 +25,8 @@
     q_hbm, k_hbm, v_hbm, g_hbm, weight_ref, bias_ref, length_ref,
     dq_ref, dk_ref, dv_ref, dw_ref, db_ref,
     raw, stage, q_t, k_t, v_t, g_t, weights, low, att, out_nat, slope, pre, upper,
-    grad_x, grad_t, grad_nat, k_nat, diffs, stage_out, back, done, tap_sum, one, two, three,
-    load_sem, own_sem, send_sem, recv_sem, block_sem, store_sem, sum_send, sum_recv,
+    grad_x, grad_t, grad_nat, k_nat, diffs, stage_out, back, tap_sum, one, two, three,
+    load_sem, own_sem, send_sem, recv_sem, block_sem, sum_send, sum_recv,
 ):
     seq_len = q_t.shape[1]
     frames = raw.shape[1]
@@ -416,22 +416,12 @@
     lax.fori_loop(0, steps, key_step, 0)
     sum_start(1, two, dp_x, x_peers, sum_end(0, one, core_peers))
 
-    stores = []
-
     def collect(which, result):
         back[which, own_rows, :] = stage_out[which, own_rows, :]
         whole = back.at[which, others, :]
         pltpu.make_async_copy(whole, whole, recv_sem.at[out_sent[which]]).wait()
         for b in range(width // WIDE):
-            done[which, :, b * WIDE : (b + 1) * WIDE] = back[which, b * WIDE : (b + 1) * WIDE, :].T
-            if (b + 1) * WIDE % quarter == 0:
-                c = b * WIDE // quarter
-                part = pl.ds(c * quarter, quarter)
-                store = pltpu.make_async_copy(
-                    done.at[which, :, part], result.at[0, :, part], store_sem.at[which, c]
-                )
-                store.start()
-                stores.append(store)
+            result[0, :, b * WIDE : (b + 1) * WIDE] = back[which, b * WIDE : (b + 1) * WIDE, :].T
 
     collect(0, dq_ref)
     sum_start(2, three, dp_y, y_peers, sum_end(1, two, x_peers))
@@ -440,8 +430,6 @@
     dw_ref[...] = sums[0:KERNEL, 0:HEAD]
     db_ref[...] = sums[KERNEL : KERNEL + 1, 0:HEAD]
     collect(1, dk_ref)
-    for store in stores:
-        store.wait()
     for i in range(1 if early else 0, len(landings) + 3):
         sent(i)
     for level, (slots, peers) in enumerate(((one, core_peers), (two, x_peers), (three, y_peers))):
@@ -449,54 +437,24 @@
         pltpu.make_async_copy(whole, whole, sum_send.at[level]).wait()
 
 
-def hand_over(*refs):
-    given, results, held, small, bias, in_sem, out_sem = refs[:5], refs[5:10], *refs[10:]
-    quarter = held.shape[2] // 4
-    copies = []
-    for i in range(3):
-        for c in range(4):
-            part = pl.ds(c * quarter, quarter)
-            where = held.at[i, :, part]
-            copies.append(
-                (
-                    pltpu.make_async_copy(given[i].at[0, :, part], where, in_sem.at[4 * i + c]),
-                    pltpu.make_async_copy(where, results[i].at[0, :, part], out_sem.at[4 * i + c]),
-                )
-            )
-    for i, where in ((3, small), (4, bias)):
-        copies.append(
-            (
-                pltpu.make_async_copy(given[i], where, in_sem.at[9 + i]),
-                pltpu.make_async_copy(where, results[i], out_sem.at[9 + i]),
-            )
-        )
-    for fetch, _ in copies:
-        fetch.start()
-    for fetch, put in copies:
-        fetch.wait()
-        put.start()
-    for _, put in copies:
-        put.wait()
-
-
 def on_device(queries, keys, values, grad_out, conv_weight, conv_bias, lengths):
     _, frames, width = queries.shape
     seq_len = frames * HEADS
     any_spec = pl.BlockSpec(memory_space=pl.ANY)
     vmem = pl.BlockSpec(memory_space=pltpu.VMEM)
-    block = jax.ShapeDtypeStruct(queries.shape, BF16)
+    landing = pltpu.VMEM(queries.shape, BF16)
     tall = seq_len + 2 * PAD
     query_grad, key_grad, value_grad, weight_grad, bias_grad = pl.pallas_call(
         core,
         out_shape=(
-            block,
-            block,
-            block,
+            landing,
+            landing,
+            landing,
             jax.ShapeDtypeStruct((KERNEL, HEAD), F32),
             jax.ShapeDtypeStruct((1, HEAD), F32),
         ),
         in_specs=[any_spec] * 4 + [vmem, vmem, pl.BlockSpec(memory_space=pltpu.SMEM)],
-        out_specs=(any_spec,) * 3 + (vmem,) * 2,
+        out_specs=(vmem,) * 5,
         scratch_shapes=[
             pltpu.VMEM((4, frames, width), BF16),
             pltpu.VMEM((4, width, frames), BF16),
@@ -518,7 +476,6 @@
             pltpu.VMEM((seq_len, seq_len), BF16),
             pltpu.VMEM((3, width, frames), BF16),
             pltpu.VMEM((3, width, frames), BF16),
-            pltpu.VMEM((3, frames, width), BF16),
             pltpu.VMEM((KERNEL + 1, 8, WIDE), F32),
             pltpu.VMEM((2, KERNEL + 1, WIDE), F32),
             pltpu.VMEM((4, KERNEL + 1, WIDE), F32),
@@ -528,7 +485,6 @@
             pltpu.SemaphoreType.DMA((7,)),
             pltpu.SemaphoreType.DMA((7,)),
             pltpu.SemaphoreType.DMA((3, HEADS)),
-            pltpu.SemaphoreType.DMA((3, 4)),
             pltpu.SemaphoreType.DMA((3,)),
             pltpu.SemaphoreType.DMA((3,)),
         ],
@@ -536,22 +492,7 @@
             collective_id=0, has_side_effects=True, vmem_limit_bytes=56 << 20
         ),
     )(queries, keys, values, grad_out, conv_weight, conv_bias, lengths)
-    found = (query_grad, key_grad, value_grad, weight_grad, bias_grad)
-    found = pl.pallas_call(
-        hand_over,
-        out_shape=tuple(jax.ShapeDtypeStruct(part.shape, part.dtype) for part in found),
-        in_specs=[any_spec] * 5,
-        out_specs=(any_spec,) * 5,
-        scratch_shapes=[
-            pltpu.VMEM((3, frames, width), BF16),
-            pltpu.VMEM((KERNEL, HEAD), F32),
-            pltpu.VMEM((1, HEAD), F32),
-            pltpu.SemaphoreType.DMA((14,)),
-            pltpu.SemaphoreType.DMA((14,)),
-        ],
-        compiler_params=pltpu.CompilerParams(vmem_limit_bytes=56 << 20),
-    )(*found)
-    return *found[:4], found[4][0]
+    return query_grad, key_grad, value_grad, weight_grad, bias_grad[0]
 
 
 def solution(mesh):

time: 94.5 us -> 94.8 us (level)
  local copies, waits for them, and re-layouts: 0 us -> 3.39 us
  Pallas kernels: 92.8 us -> 89.8 us
    unnamed x0 -> x9, local copies, waits for them, and re-layouts: none -> 3.39 us
    pallas_call x2 -> x1, Pallas kernels: 92.8 us -> 89.8 us  [on_device(): pl.pallas_call(core, out_shape=(landing, landing, landing, jax.ShapeDtype...]
where the time goes in v4:
time: 94.8 us; the launch traced here: 94.5 us
  Pallas kernels  89.8 us (95%)
  local copies, waits for them, and re-layouts  3.39 us (4%)
  between operations  1.29 us (1%)
    pallas_call x1, Pallas kernels, on_device(): pl.pallas_call(core, out_shape=(landing, landing, landing, jax.ShapeDtype...  89.8 us
    unnamed x9, local copies, waits for them, and re-layouts  3.39 us

profile of v4, /device:TPU:1, one launch (start us, length us, event | category | flops | bytes accessed | tf_op | source)
XLA Modules:
  0.0 94.5 jit_solution(3066933505708320373)
XLA Ops:
  1.3 89.8 %shard_map.110 = (bf16[1,128,1536]{2,1,0:T(8,128)(2,1)S(1)}, bf16[1,128,1536]{2,1,0:T(8,128)(2,1)S(1)}, bf16[1,128,1536]{2,1,0:T(8,128)(2,1)S(1)}, f32[31,96]{1,0:T(8,128)}, f32[1,96]{1,0:T(1,128)}) custom-call(bf16[1,128,1536]{2,1,0:T(8,128)(2,1)} %q_hbm.1, bf16[1,128,1536]{2,1,0:T(8,128)(2,1)} %k_hbm.1, bf16[1,128,1536]{2,1,0:T(8,128)(2,1)} %v_hbm.1, ...), custom_call_target="tpu_custom_call" | custom-call | tf_op jit(solution)/shard_map/pallas_call | solution.py:447
  91.1 0.7 copy.17
  91.9 0.7 copy.18
  92.6 0.0 copy-start
  92.6 0.7 copy.19
  93.4 0.0 copy-done
  93.4 0.0 copy-start.1
  93.4 0.6 copy.21
  94.0 0.0 copy-done.1
  94.0 0.5 copy.22
Async XLA Ops:
  92.6 0.8 copy-start
  93.4 0.6 copy-start.1
